TPU v7x, 512 devices: a whole 4x4x16 slice. The times are simulated.
512 devices in a mesh: gx: 64 (over x, z_lo, core), gy: 8 (over z_hi, y).
Axes of the slice: x: 4, y: 4, z: 16 (z_hi: 2, z_lo: 8; z = z_hi * 8 + z_lo), core: 2. Of those that a mesh axis runs over, the one named last changes fastest.
Arguments:
- species: float32 [8, 16, 1024, 1024], P(None, None, 'gx', 'gy'), may hold values from 0.1 to 2
- porosity: float32 [16, 1024, 1024], P(None, 'gx', 'gy'), may hold values from 0.15 to 0.35
- pressure_old: float32 [16, 1024, 1024], P(None, 'gx', 'gy'), may hold values from -6 to 6
- source: float32 [16, 1024, 1024], P(None, 'gx', 'gy'), may hold values from -2 to 2
- zone_label: int32 [16, 1024, 1024], P(None, 'gx', 'gy'), may hold values from 0 to 3
- fixed_cell: int32 [16, 1024, 1024], P(None, 'gx', 'gy'), may hold values 0 or 1
Outputs:
- concentration: float32 [8, 16, 1024, 1024], P(None, None, 'gx', 'gy')
- pressure: float32 [16, 1024, 1024], P(None, 'gx', 'gy')
- porosity_next: float32 [16, 1024, 1024], P(None, 'gx', 'gy')
Inputs may be any that keep to these rules, and one draw needn't show every extreme that they name: `zone_label`: one of four mineral zones.
All inputs are finite; a program needn't handle non-finite values. No bound on the sum of `fixed_cell` on one device may be relied on, other than what follows from the above.
Results may differ from a plain program's by a relative error of at most 0.0003.
Values sent between devices are 32-bit elements; how exact they have to be, the bound alone decides.
A program may use at most 128 MiB of HBM per device.

v0:
```python
import math

import jax
import jax.numpy as jnp
from jax import lax
from jax.sharding import PartitionSpec as P

SWEEPS = 3


ZONE_RATES = (0.02, 0.05, 0.1, 0.2)
ZONE_PERMEABILITY = (5.0, 10.0, 20.0, 40.0)
SOLUBILITY = 0.5
MOLAR_VOLUME = 0.05
STORAGE_COEF = 0.2
TIME_STEP = 0.2
CHEB_SPREAD = 0.92
STOICHIOMETRY = (-1.0, -1.0, 0.0, 0.0, 0.0, 0.0, 0.0, 0.0)


def with_halo(x, sides, width):
    for axis, dim in sides:
        devices, length = (lax.axis_size(axis), x.shape[dim])
        up = [(i, (i + 1) % devices) for i in range(devices - 1)]
        down = [(j, i) for i, j in up]
        last = lax.slice_in_dim(x, length - width, length, axis=dim)
        first = lax.slice_in_dim(x, 0, width, axis=dim)
        before = lax.ppermute(last, axis, up)
        after = lax.ppermute(first, axis, down)
        x = jnp.concatenate([before, x, after], axis=dim)
    return x


def lookup(labels, table):
    total = jnp.zeros(labels.shape, jnp.float32)
    for label_level, level_value in enumerate(table):
        total = total + jnp.where(labels == label_level, jnp.float32(level_value), jnp.float32(0.0))
    return total


def beside_all(extended):
    centre = extended[..., 1:-1, 1:-1]
    widths = [(0, 0)] * (centre.ndim - 3) + [(1, 1), (0, 0), (0, 0)]
    zpadded = jnp.pad(centre, widths)
    sides = [
        extended[..., :-2, 1:-1],
        extended[..., 2:, 1:-1],
        extended[..., 1:-1, :-2],
        extended[..., 1:-1, 2:],
        zpadded[..., :-2, :, :],
        zpadded[..., 2:, :, :],
    ]
    return (centre, sides)


def harmonic_safe(first, second):
    summed = first + second
    positive = summed > 0
    return jnp.where(positive, 2.0 * first * second / jnp.where(positive, summed, 1.0), 0.0)


def face_terms(perm_ext):
    centre, sides = beside_all(perm_ext)
    return [harmonic_safe(centre, beside) for beside in sides]


def diagonal_of(storage, transmit):
    total = storage
    for term in transmit:
        total = total + term
    return total


def apply_operator(pressure_ext, transmit, storage):
    centre, sides = beside_all(pressure_ext)
    applied = storage * centre
    for term, beside in zip(transmit, sides):
        applied = applied + term * (centre - beside)
    return applied


def relax_weight(iteration):
    return 1.0 / (1.0 + CHEB_SPREAD * math.cos(math.pi * (2 * iteration + 1) / (2 * SWEEPS)))


def rim_pressure(pressure):
    return with_halo(pressure, (("gx", 1), ("gy", 2)), 1)


def shards(species, porosity, pressure_old, source, zone_label, fixed_cell):
    reaction = lookup(zone_label, ZONE_RATES) * (species[0] * species[1] - SOLUBILITY)
    porosity_next = porosity - MOLAR_VOLUME * reaction
    permeab = lookup(zone_label, ZONE_PERMEABILITY) * porosity_next**3 / (1.0 - porosity_next) ** 2
    storage = STORAGE_COEF * porosity_next
    rhs_field = storage * pressure_old + source
    free_mask = 1.0 - fixed_cell.astype(jnp.float32)
    species_ext = with_halo(species, (("gx", 2), ("gy", 3)), 1)
    perm_ext = with_halo(permeab, (("gx", 1), ("gy", 2)), 1)
    start_ext = rim_pressure(pressure_old)
    transmit = face_terms(perm_ext)
    diagonal_sum = diagonal_of(storage, transmit)
    pressure = pressure_old
    for iteration in range(SWEEPS):
        current_ext = start_ext if iteration == 0 else rim_pressure(pressure)
        residual = (rhs_field - apply_operator(current_ext, transmit, storage)) * free_mask
        pressure = pressure + relax_weight(iteration) * residual / diagonal_sum
    pressure_ext = rim_pressure(pressure)
    flow_centre, flow_sides = beside_all(pressure_ext)
    centre_c, sides_c = beside_all(species_ext)
    change = jnp.zeros(species.shape, jnp.float32)
    for term, beside_p, beside_c in zip(transmit, flow_sides, sides_c):
        outflow = term * (flow_centre - beside_p)
        change = change + outflow * jnp.where(outflow > 0, centre_c, beside_c)
    stoich = jnp.array(STOICHIOMETRY, jnp.float32)[:, None, None, None]
    concentration = species - TIME_STEP / porosity_next * change + stoich * reaction
    return (concentration, flow_centre, porosity_next)


def solution(mesh):
    in_specs = (
        P(None, None, "gx", "gy"),
        P(None, "gx", "gy"),
        P(None, "gx", "gy"),
        P(None, "gx", "gy"),
        P(None, "gx", "gy"),
        P(None, "gx", "gy"),
    )
    out_specs = (P(None, None, "gx", "gy"), P(None, "gx", "gy"), P(None, "gx", "gy"))
    return jax.shard_map(shards, mesh=mesh, in_specs=in_specs, out_specs=out_specs, check_vma=False)
```

profile of v0, /device:TPU:30, one launch (start us, length us, event | category | flops | bytes accessed | tf_op | source)
XLA Modules:
  0.0 263.0 jit_solution(4359639166974590691)
XLA Ops:
  1.7 12.9 %collective-permute-start.3 = (f32[16,1,128]{2,1,0:T(1,128)S(1)}, f32[16,1,128]{2,1,0:T(1,128)S(1)}, u32[]{:S(2)}, u32[]{:S(2)}) collective-permute-start(f32[16,1,128]{2,1,0:T(1,128)S(1)} %get-tuple-element.67), channel_id=1, source_target_pairs={{8,0},{16,8},{24,16},{32,24},{40,32},{48,40},{56,48},{64,56},{72,6... | collective-permute-start | bytes 24584 | tf_op jit(solution)/shard_map/ppermute | solution.py:29
  14.5 1.9 collective-permute-start.1
  16.5 1.9 broadcast_divide_fusion
  18.5 1.9 collective-permute-start
  20.5 11.1 %collective-permute-start.2 = (f32[16,1,128]{2,1,0:T(1,128)S(1)}, f32[16,1,128]{2,1,0:T(1,128)S(1)}, u32[]{:S(2)}, u32[]{:S(2)}) collective-permute-start(f32[16,1,128]{2,1,0:T(1,128)S(1)} %get-tuple-element.64), channel_id=1, source_target_pairs={{8,0},{16,8},{24,16},{32,24},{40,32},{48,40},{56,48},{64,56},{72,6... | collective-permute-start | bytes 24584 | tf_op jit(solution)/shard_map/ppermute | solution.py:29
  32.7 2.7 %collective-permute-start.7 = (f32[16,18,1]{2,1,0:T(8,128)S(1)}, f32[16,18,1]{2,1,0:T(8,128)S(1)}, u32[]{:S(2)}, u32[]{:S(2)}) collective-permute-start(f32[16,18,1]{2,1,0:T(8,128)S(1)} %get-tuple-element.51), channel_id=1, source_target_pairs={{1,0},{2,1},{3,2},{4,3},{5,4},{6,5},{7,6},{9,8},{10,9},{11,10},{12... | collective-permute-start | bytes 3464 | tf_op jit(solution)/shard_map/ppermute | solution.py:29
  35.4 14.0 %collective-permute-start.5 = (f32[16,18,1]{2,1,0:T(8,128)S(1)}, f32[16,18,1]{2,1,0:T(8,128)S(1)}, u32[]{:S(2)}, u32[]{:S(2)}) collective-permute-start(f32[16,18,1]{2,1,0:T(8,128)S(1)} %get-tuple-element.50), channel_id=1, source_target_pairs={{0,1},{1,2},{2,3},{3,4},{4,5},{5,6},{6,7},{8,9},{9,10},{10,11},{11... | collective-permute-start | bytes 3464 | tf_op jit(solution)/shard_map/ppermute | solution.py:28
  49.6 1.9 collective-permute-start.4
  51.5 3.9 %collective-permute-start.6 = (f32[16,18,1]{2,1,0:T(8,128)S(1)}, f32[16,18,1]{2,1,0:T(8,128)S(1)}, u32[]{:S(2)}, u32[]{:S(2)}) collective-permute-start(f32[16,18,1]{2,1,0:T(8,128)S(1)} %get-tuple-element.48), channel_id=1, source_target_pairs={{1,0},{2,1},{3,2},{4,3},{5,4},{6,5},{7,6},{9,8},{10,9},{11,10},{12... | collective-permute-start | bytes 3464 | tf_op jit(solution)/shard_map/ppermute | solution.py:29
  57.1 12.8 %collective-permute-done.6 = f32[16,18,1]{2,1,0:T(8,128)S(1)} collective-permute-done((f32[16,18,1]{2,1,0:T(8,128)S(1)}, f32[16,18,1]{2,1,0:T(8,128)S(1)}, u32[]{:S(2)}, u32[]{:S(2)}) %collective-permute-start.6) | collective-permute-done | bytes 1184 | tf_op jit(solution)/shard_map/ppermute | solution.py:29
  69.9 2.0 fusion.28
  71.9 2.1 collective-permute-start.9
  74.0 2.3 collective-permute-start.8
  76.3 10.2 %collective-permute-done.8 = f32[16,1,128]{2,1,0:T(1,128)S(1)} collective-permute-done((f32[16,1,128]{2,1,0:T(1,128)S(1)}, f32[16,1,128]{2,1,0:T(1,128)S(1)}, u32[]{:S(2)}, u32[]{:S(2)}) %collective-permute-start.8) | collective-permute-done | bytes 8224 | tf_op jit(solution)/shard_map/ppermute | solution.py:28
  88.6 14.7 %collective-permute-start.10 = (f32[16,18,1]{2,1,0:T(8,128)S(1)}, f32[16,18,1]{2,1,0:T(8,128)S(1)}, u32[]{:S(2)}, u32[]{:S(2)}) collective-permute-start(f32[16,18,1]{2,1,0:T(8,128)S(1)} %get-tuple-element.46), channel_id=1, source_target_pairs={{0,1},{1,2},{2,3},{3,4},{4,5},{5,6},{6,7},{8,9},{9,10},{10,11},{11... | collective-permute-start | bytes 3464 | tf_op jit(solution)/shard_map/ppermute | solution.py:28
  107.9 2.1 collective-permute-start.13
  110.0 2.4 collective-permute-start.12
  112.4 10.0 %collective-permute-done.12 = f32[16,1,128]{2,1,0:T(1,128)S(1)} collective-permute-done((f32[16,1,128]{2,1,0:T(1,128)S(1)}, f32[16,1,128]{2,1,0:T(1,128)S(1)}, u32[]{:S(2)}, u32[]{:S(2)}) %collective-permute-start.12) | collective-permute-done | bytes 8224 | tf_op jit(solution)/shard_map/ppermute | solution.py:28
  124.5 15.3 %collective-permute-start.14 = (f32[16,18,1]{2,1,0:T(8,128)S(1)}, f32[16,18,1]{2,1,0:T(8,128)S(1)}, u32[]{:S(2)}, u32[]{:S(2)}) collective-permute-start(f32[16,18,1]{2,1,0:T(8,128)S(1)} %get-tuple-element.44), channel_id=1, source_target_pairs={{0,1},{1,2},{2,3},{3,4},{4,5},{5,6},{6,7},{8,9},{9,10},{10,11},{11... | collective-permute-start | bytes 3464 | tf_op jit(solution)/shard_map/ppermute | solution.py:28
  145.4 11.1 %collective-permute-start.18 = (f32[16,1,128]{2,1,0:T(1,128)S(1)}, f32[16,1,128]{2,1,0:T(1,128)S(1)}, u32[]{:S(2)}, u32[]{:S(2)}) collective-permute-start(f32[16,1,128]{2,1,0:T(1,128)S(1)} %get-tuple-element.59), channel_id=1, source_target_pairs={{8,0},{16,8},{24,16},{32,24},{40,32},{48,40},{56,48},{64,56},{72,6... | collective-permute-start | bytes 24584 | tf_op jit(solution)/shard_map/ppermute | solution.py:29
  161.3 11.1 %collective-permute-start.19 = (f32[8,16,1,128]{3,1,2,0:T(8,128)}, f32[8,16,1,128]{3,1,2,0:T(8,128)}, u32[]{:S(2)}, u32[]{:S(2)}) collective-permute-start(f32[8,16,1,128]{3,1,2,0:T(8,128)} %get-tuple-element.39), channel_id=1, source_target_pairs={{8,0},{16,8},{24,16},{32,24},{40,32},{48,40},{56,48},{64,56},{72,6... | collective-permute-start | bytes 196616 | tf_op jit(solution)/shard_map/ppermute | solution.py:29
  172.4 1.9 collective-permute-start.17
  174.3 5.0 %copy.84 = f32[8,16,16,128]{2,1,3,0:T(8,128)} copy(f32[8,16,16,128]{3,2,1,0:T(8,128)S(1)} %copy-done.1) | data formatting | bytes 2097152 | tf_op args[0]
  181.0 15.4 %collective-permute-start.20 = (f32[16,18,1]{2,1,0:T(8,128)}, f32[16,18,1]{2,1,0:T(8,128)S(1)}, u32[]{:S(2)}, u32[]{:S(2)}) collective-permute-start(f32[16,18,1]{2,1,0:T(8,128)} %get-tuple-element.42), channel_id=1, source_target_pairs={{0,1},{1,2},{2,3},{3,4},{4,5},{5,6},{6,7},{8,9},{9,10},{10,11},{11... | collective-permute-start | bytes 3464 | tf_op jit(solution)/shard_map/ppermute | solution.py:28
  197.8 5.7 %copy.85 = f32[8,16,1,128]{2,1,3,0:T(8,128)} copy(f32[8,16,1,128]{3,1,2,0:T(8,128)} %collective-permute-done.19) | data formatting | bytes 131072 | tf_op jit(solution)/shard_map/ppermute | solution.py:29
  203.5 5.7 %copy.83 = f32[8,16,1,128]{2,1,3,0:T(8,128)} copy(f32[8,16,1,128]{3,1,2,0:T(8,128)} %collective-permute-done.17) | data formatting | bytes 131072 | tf_op jit(solution)/shard_map/ppermute | solution.py:28
  209.2 10.5 %pad_maximum_fusion = f32[8,16,18,128]{2,1,3,0:T(8,128)S(1)} fusion(f32[8,16,1,128]{2,1,3,0:T(8,128)} %copy.85, f32[8,16,16,128]{2,1,3,0:T(8,128)} %copy.84, f32[8,16,1,128]{2,1,3,0:T(8,128)} %copy.83), kind=kLoop, calls=%fused_computation | loop fusion | flops 589824 | bytes 2359296 | tf_op jit(solution)/shard_map/concatenate | solution.py:30
  219.8 3.3 %copy-done = f32[8,16,18,128]{2,1,3,0:T(8,128)} copy-done((f32[8,16,18,128]{2,1,3,0:T(8,128)}, f32[8,16,18,128]{2,1,3,0:T(8,128)S(1)}, u32[]{:S(2)}) %copy-start) | copy-done | bytes 1179672
  225.6 14.9 %collective-permute-start.21 = (f32[8,16,18,1]{2,1,3,0:T(8,128)}, f32[8,16,18,1]{2,1,3,0:T(8,128)}, u32[]{:S(2)}, u32[]{:S(2)}) collective-permute-start(f32[8,16,18,1]{2,1,3,0:T(8,128)} %get-tuple-element.36), channel_id=1, source_target_pairs={{0,1},{1,2},{2,3},{3,4},{4,5},{5,6},{6,7},{8,9},{9,10},{10,11},{11... | collective-permute-start | bytes 27656 | tf_op jit(solution)/shard_map/ppermute | solution.py:28
  248.7 5.8 %copy.87 = f32[8,16,18,128]{3,1,2,0:T(8,128)S(1)} copy(f32[8,16,18,128]{2,1,3,0:T(8,128)} %copy-done) | data formatting | bytes 2359296 | tf_op jit(solution)/shard_map/concatenate | solution.py:30
  256.2 2.8 %copy.86 = f32[8,16,18,1]{3,1,2,0:T(8,128)} copy(f32[8,16,18,1]{2,1,3,0:T(8,128)} %collective-permute-done.21) | data formatting | bytes 18432 | tf_op jit(solution)/shard_map/ppermute | solution.py:28
  259.0 2.7 %fusion.6 = f32[8,16,16,128]{3,1,2,0:T(8,128)S(1)} fusion(f32[8,16,16,128]{3,1,2,0:T(8,128)S(1)} %copy.101, f32[8,16,18,1]{3,1,2,0:T(8,128)S(1)} %copy.92, f32[8,16,18,128]{3,1,2,0:T(8,128)S(1)} %copy.87, f32[8,16,18,1]{3,1,2,0:T(8,128)} %copy.86, f32[8,16,1,128]{3,1,2,0:T(8,128)} %collective-permute-done.19, f32[8,16,1,128]{3,1,2,0:T(8,128)} %collective-permute-done.17, ...), kind=kLoop, calls=%fused_computation.9 | loop fusion | flops 6553600 | bytes 4671520 | tf_op jit(solution)/shard_map/add | solution.py:115
  (90 shorter events, 39.5 us)
Async XLA Ops:
  0.6 142.4 %copy-start.3 = (f32[16,16,128]{2,1,0:T(8,128)S(1)}, f32[16,16,128]{2,1,0:T(8,128)}, u32[]{:S(2)}) copy-start(f32[16,16,128]{2,1,0:T(8,128)} %param.9) | copy-start | bytes 393220
  0.6 155.9 %copy-start.1 = (f32[8,16,16,128]{3,2,1,0:T(8,128)S(1)}, f32[8,16,16,128]{3,2,1,0:T(8,128)}, u32[]{:S(2)}) copy-start(f32[8,16,16,128]{3,2,1,0:T(8,128)} %param.7) | copy-start | bytes 3145732
  0.7 142.4 %copy-start.5 = (s32[16,16,128]{2,1,0:T(8,128)S(1)}, s32[16,16,128]{2,1,0:T(8,128)}, u32[]{:S(2)}) copy-start(s32[16,16,128]{2,1,0:T(8,128)} %param.12) | copy-start | bytes 393220
  0.7 142.4 %copy-start.6 = (f32[16,16,128]{2,1,0:T(8,128)S(1)}, f32[16,16,128]{2,1,0:T(8,128)}, u32[]{:S(2)}) copy-start(f32[16,16,128]{2,1,0:T(8,128)} %param.10) | copy-start | bytes 393220
  1.7 29.9 %collective-permute-start.3 = (f32[16,1,128]{2,1,0:T(1,128)S(1)}, f32[16,1,128]{2,1,0:T(1,128)S(1)}, u32[]{:S(2)}, u32[]{:S(2)}) collective-permute-start(f32[16,1,128]{2,1,0:T(1,128)S(1)} %get-tuple-element.67), channel_id=1, source_target_pairs={{8,0},{16,8},{24,16},{32,24},{40,32},{48,40},{56,48},{64,56},{72,6... | collective-permute-start | bytes 24584 | tf_op jit(solution)/shard_map/ppermute | solution.py:29
  14.5 17.1 %collective-permute-start.1 = (f32[16,1,128]{2,1,0:T(1,128)S(1)}, f32[16,1,128]{2,1,0:T(1,128)S(1)}, u32[]{:S(2)}, u32[]{:S(2)}) collective-permute-start(f32[16,1,128]{2,1,0:T(1,128)S(1)} %get-tuple-element.66), channel_id=1, source_target_pairs={{0,8},{8,16},{16,24},{24,32},{32,40},{40,48},{48,56},{56,64},{64,7... | collective-permute-start | bytes 24584 | tf_op jit(solution)/shard_map/ppermute | solution.py:28
  18.4 160.9 %copy-start.2 = (f32[16,16,128]{2,1,0:T(8,128)}, f32[16,16,128]{2,1,0:T(8,128)S(1)}, u32[]{:S(2)}) copy-start(f32[16,16,128]{2,1,0:T(8,128)S(1)} %get-tuple-element.25) | copy-start | bytes 393220
  18.5 30.8 %collective-permute-start = (f32[16,1,128]{2,1,0:T(1,128)S(1)}, f32[16,1,128]{2,1,0:T(1,128)S(1)}, u32[]{:S(2)}, u32[]{:S(2)}) collective-permute-start(f32[16,1,128]{2,1,0:T(1,128)S(1)} %get-tuple-element.65), channel_id=1, source_target_pairs={{0,8},{8,16},{16,24},{24,32},{32,40},{40,48},{48,56},{56,64},{64,7... | collective-permute-start | bytes 24584 | tf_op jit(solution)/shard_map/ppermute | solution.py:28
  20.5 28.9 %collective-permute-start.2 = (f32[16,1,128]{2,1,0:T(1,128)S(1)}, f32[16,1,128]{2,1,0:T(1,128)S(1)}, u32[]{:S(2)}, u32[]{:S(2)}) collective-permute-start(f32[16,1,128]{2,1,0:T(1,128)S(1)} %get-tuple-element.64), channel_id=1, source_target_pairs={{8,0},{16,8},{24,16},{32,24},{40,32},{48,40},{56,48},{64,56},{72,6... | collective-permute-start | bytes 24584 | tf_op jit(solution)/shard_map/ppermute | solution.py:29
  32.7 22.7 %collective-permute-start.7 = (f32[16,18,1]{2,1,0:T(8,128)S(1)}, f32[16,18,1]{2,1,0:T(8,128)S(1)}, u32[]{:S(2)}, u32[]{:S(2)}) collective-permute-start(f32[16,18,1]{2,1,0:T(8,128)S(1)} %get-tuple-element.51), channel_id=1, source_target_pairs={{1,0},{2,1},{3,2},{4,3},{5,4},{6,5},{7,6},{9,8},{10,9},{11,10},{12... | collective-permute-start | bytes 3464 | tf_op jit(solution)/shard_map/ppermute | solution.py:29
  35.4 20.1 %collective-permute-start.5 = (f32[16,18,1]{2,1,0:T(8,128)S(1)}, f32[16,18,1]{2,1,0:T(8,128)S(1)}, u32[]{:S(2)}, u32[]{:S(2)}) collective-permute-start(f32[16,18,1]{2,1,0:T(8,128)S(1)} %get-tuple-element.50), channel_id=1, source_target_pairs={{0,1},{1,2},{2,3},{3,4},{4,5},{5,6},{6,7},{8,9},{9,10},{10,11},{11... | collective-permute-start | bytes 3464 | tf_op jit(solution)/shard_map/ppermute | solution.py:28
  49.6 7.6 %collective-permute-start.4 = (f32[16,18,1]{2,1,0:T(8,128)S(1)}, f32[16,18,1]{2,1,0:T(8,128)S(1)}, u32[]{:S(2)}, u32[]{:S(2)}) collective-permute-start(f32[16,18,1]{2,1,0:T(8,128)S(1)} %get-tuple-element.49), channel_id=1, source_target_pairs={{0,1},{1,2},{2,3},{3,4},{4,5},{5,6},{6,7},{8,9},{9,10},{10,11},{11... | collective-permute-start | bytes 3464 | tf_op jit(solution)/shard_map/ppermute | solution.py:28
  51.5 18.4 %collective-permute-start.6 = (f32[16,18,1]{2,1,0:T(8,128)S(1)}, f32[16,18,1]{2,1,0:T(8,128)S(1)}, u32[]{:S(2)}, u32[]{:S(2)}) collective-permute-start(f32[16,18,1]{2,1,0:T(8,128)S(1)} %get-tuple-element.48), channel_id=1, source_target_pairs={{1,0},{2,1},{3,2},{4,3},{5,4},{6,5},{7,6},{9,8},{10,9},{11,10},{12... | collective-permute-start | bytes 3464 | tf_op jit(solution)/shard_map/ppermute | solution.py:29
  71.9 4.3 %collective-permute-start.9 = (f32[16,1,128]{2,1,0:T(1,128)S(1)}, f32[16,1,128]{2,1,0:T(1,128)S(1)}, u32[]{:S(2)}, u32[]{:S(2)}) collective-permute-start(f32[16,1,128]{2,1,0:T(1,128)S(1)} %get-tuple-element.63), channel_id=1, source_target_pairs={{8,0},{16,8},{24,16},{32,24},{40,32},{48,40},{56,48},{64,56},{72,6... | collective-permute-start | bytes 24584 | tf_op jit(solution)/shard_map/ppermute | solution.py:29
  74.0 12.5 %collective-permute-start.8 = (f32[16,1,128]{2,1,0:T(1,128)S(1)}, f32[16,1,128]{2,1,0:T(1,128)S(1)}, u32[]{:S(2)}, u32[]{:S(2)}) collective-permute-start(f32[16,1,128]{2,1,0:T(1,128)S(1)} %get-tuple-element.62), channel_id=1, source_target_pairs={{0,8},{8,16},{16,24},{24,32},{32,40},{40,48},{48,56},{56,64},{64,7... | collective-permute-start | bytes 24584 | tf_op jit(solution)/shard_map/ppermute | solution.py:28
  86.6 18.4 %collective-permute-start.11 = (f32[16,18,1]{2,1,0:T(8,128)S(1)}, f32[16,18,1]{2,1,0:T(8,128)S(1)}, u32[]{:S(2)}, u32[]{:S(2)}) collective-permute-start(f32[16,18,1]{2,1,0:T(8,128)S(1)} %get-tuple-element.47), channel_id=1, source_target_pairs={{1,0},{2,1},{3,2},{4,3},{5,4},{6,5},{7,6},{9,8},{10,9},{11,10},{12... | collective-permute-start | bytes 3464 | tf_op jit(solution)/shard_map/ppermute | solution.py:29
  88.6 17.9 %collective-permute-start.10 = (f32[16,18,1]{2,1,0:T(8,128)S(1)}, f32[16,18,1]{2,1,0:T(8,128)S(1)}, u32[]{:S(2)}, u32[]{:S(2)}) collective-permute-start(f32[16,18,1]{2,1,0:T(8,128)S(1)} %get-tuple-element.46), channel_id=1, source_target_pairs={{0,1},{1,2},{2,3},{3,4},{4,5},{5,6},{6,7},{8,9},{9,10},{10,11},{11... | collective-permute-start | bytes 3464 | tf_op jit(solution)/shard_map/ppermute | solution.py:28
  107.9 72.4 %copy-start.7 = (f32[16,16,128]{2,1,0:T(8,128)S(1)}, f32[16,16,128]{2,1,0:T(8,128)}, u32[]{:S(2)}) copy-start(f32[16,16,128]{2,1,0:T(8,128)} %get-tuple-element.24) | copy-start | bytes 393220
  107.9 4.5 %collective-permute-start.13 = (f32[16,1,128]{2,1,0:T(1,128)S(1)}, f32[16,1,128]{2,1,0:T(1,128)S(1)}, u32[]{:S(2)}, u32[]{:S(2)}) collective-permute-start(f32[16,1,128]{2,1,0:T(1,128)S(1)} %get-tuple-element.61), channel_id=1, source_target_pairs={{8,0},{16,8},{24,16},{32,24},{40,32},{48,40},{56,48},{64,56},{72,6... | collective-permute-start | bytes 24584 | tf_op jit(solution)/shard_map/ppermute | solution.py:29
  110.0 12.5 %collective-permute-start.12 = (f32[16,1,128]{2,1,0:T(1,128)S(1)}, f32[16,1,128]{2,1,0:T(1,128)S(1)}, u32[]{:S(2)}, u32[]{:S(2)}) collective-permute-start(f32[16,1,128]{2,1,0:T(1,128)S(1)} %get-tuple-element.60), channel_id=1, source_target_pairs={{0,8},{8,16},{16,24},{24,32},{32,40},{40,48},{48,56},{56,64},{64,7... | collective-permute-start | bytes 24584 | tf_op jit(solution)/shard_map/ppermute | solution.py:28
  122.6 19.0 %collective-permute-start.15 = (f32[16,18,1]{2,1,0:T(8,128)S(1)}, f32[16,18,1]{2,1,0:T(8,128)S(1)}, u32[]{:S(2)}, u32[]{:S(2)}) collective-permute-start(f32[16,18,1]{2,1,0:T(8,128)S(1)} %get-tuple-element.45), channel_id=1, source_target_pairs={{1,0},{2,1},{3,2},{4,3},{5,4},{6,5},{7,6},{9,8},{10,9},{11,10},{12... | collective-permute-start | bytes 3464 | tf_op jit(solution)/shard_map/ppermute | solution.py:29
  124.5 18.5 %collective-permute-start.14 = (f32[16,18,1]{2,1,0:T(8,128)S(1)}, f32[16,18,1]{2,1,0:T(8,128)S(1)}, u32[]{:S(2)}, u32[]{:S(2)}) collective-permute-start(f32[16,18,1]{2,1,0:T(8,128)S(1)} %get-tuple-element.44), channel_id=1, source_target_pairs={{0,1},{1,2},{2,3},{3,4},{4,5},{5,6},{6,7},{8,9},{9,10},{10,11},{11... | collective-permute-start | bytes 3464 | tf_op jit(solution)/shard_map/ppermute | solution.py:28
  143.4 97.2 %copy-start.4 = (f32[16,16,128]{2,1,0:T(8,128)}, f32[16,16,128]{2,1,0:T(8,128)S(1)}, u32[]{:S(2)}) copy-start(f32[16,16,128]{2,1,0:T(8,128)S(1)} %fusion.49) | copy-start | bytes 393220
  143.4 13.4 %collective-permute-start.16 = (f32[16,1,128]{2,1,0:T(1,128)S(1)}, f32[16,1,128]{2,1,0:T(1,128)S(1)}, u32[]{:S(2)}, u32[]{:S(2)}) collective-permute-start(f32[16,1,128]{2,1,0:T(1,128)S(1)} %get-tuple-element.58), channel_id=1, source_target_pairs={{0,8},{8,16},{16,24},{24,32},{32,40},{40,48},{48,56},{56,64},{64,7... | collective-permute-start | bytes 24584 | tf_op jit(solution)/shard_map/ppermute | solution.py:28
  145.4 12.5 %collective-permute-start.18 = (f32[16,1,128]{2,1,0:T(1,128)S(1)}, f32[16,1,128]{2,1,0:T(1,128)S(1)}, u32[]{:S(2)}, u32[]{:S(2)}) collective-permute-start(f32[16,1,128]{2,1,0:T(1,128)S(1)} %get-tuple-element.59), channel_id=1, source_target_pairs={{8,0},{16,8},{24,16},{32,24},{40,32},{48,40},{56,48},{64,56},{72,6... | collective-permute-start | bytes 24584 | tf_op jit(solution)/shard_map/ppermute | solution.py:29
  156.9 39.6 %copy-start.8 = (f32[16,1,128]{2,1,0:T(1,128)}, f32[16,1,128]{2,1,0:T(1,128)S(1)}, u32[]{:S(2)}) copy-start(f32[16,1,128]{2,1,0:T(1,128)S(1)} %collective-permute-done.16) | copy-start | bytes 24580
  158.7 37.8 %collective-permute-start.22 = (f32[16,18,1]{2,1,0:T(8,128)}, f32[16,18,1]{2,1,0:T(8,128)}, u32[]{:S(2)}, u32[]{:S(2)}) collective-permute-start(f32[16,18,1]{2,1,0:T(8,128)} %get-tuple-element.43), channel_id=1, source_target_pairs={{1,0},{2,1},{3,2},{4,3},{5,4},{6,5},{7,6},{9,8},{10,9},{11,10},{12... | collective-permute-start | bytes 3464 | tf_op jit(solution)/shard_map/ppermute | solution.py:29
  161.3 36.5 %collective-permute-start.19 = (f32[8,16,1,128]{3,1,2,0:T(8,128)}, f32[8,16,1,128]{3,1,2,0:T(8,128)}, u32[]{:S(2)}, u32[]{:S(2)}) collective-permute-start(f32[8,16,1,128]{3,1,2,0:T(8,128)} %get-tuple-element.39), channel_id=1, source_target_pairs={{8,0},{16,8},{24,16},{32,24},{40,32},{48,40},{56,48},{64,56},{72,6... | collective-permute-start | bytes 196616 | tf_op jit(solution)/shard_map/ppermute | solution.py:29
  172.4 31.1 %collective-permute-start.17 = (f32[8,16,1,128]{3,1,2,0:T(8,128)}, f32[8,16,1,128]{3,1,2,0:T(8,128)}, u32[]{:S(2)}, u32[]{:S(2)}) collective-permute-start(f32[8,16,1,128]{3,1,2,0:T(8,128)} %get-tuple-element.38), channel_id=1, source_target_pairs={{0,8},{8,16},{16,24},{24,32},{32,40},{40,48},{48,56},{56,64},{64,7... | collective-permute-start | bytes 196616 | tf_op jit(solution)/shard_map/ppermute | solution.py:28
  181.0 59.5 %collective-permute-start.20 = (f32[16,18,1]{2,1,0:T(8,128)}, f32[16,18,1]{2,1,0:T(8,128)S(1)}, u32[]{:S(2)}, u32[]{:S(2)}) collective-permute-start(f32[16,18,1]{2,1,0:T(8,128)} %get-tuple-element.42), channel_id=1, source_target_pairs={{0,1},{1,2},{2,3},{3,4},{4,5},{5,6},{6,7},{8,9},{9,10},{10,11},{11... | collective-permute-start | bytes 3464 | tf_op jit(solution)/shard_map/ppermute | solution.py:28
  223.7 30.8 %collective-permute-start.23 = (f32[8,16,18,1]{2,1,3,0:T(8,128)S(1)}, f32[8,16,18,1]{2,1,3,0:T(8,128)}, u32[]{:S(2)}, u32[]{:S(2)}) collective-permute-start(f32[8,16,18,1]{2,1,3,0:T(8,128)S(1)} %get-tuple-element.37), channel_id=1, source_target_pairs={{1,0},{2,1},{3,2},{4,3},{5,4},{6,5},{7,6},{9,8},{10,9},{11,10},{12... | collective-permute-start | bytes 27656 | tf_op jit(solution)/shard_map/ppermute | solution.py:29
  225.6 30.6 %collective-permute-start.21 = (f32[8,16,18,1]{2,1,3,0:T(8,128)}, f32[8,16,18,1]{2,1,3,0:T(8,128)}, u32[]{:S(2)}, u32[]{:S(2)}) collective-permute-start(f32[8,16,18,1]{2,1,3,0:T(8,128)} %get-tuple-element.36), channel_id=1, source_target_pairs={{0,1},{1,2},{2,3},{3,4},{4,5},{5,6},{6,7},{8,9},{9,10},{10,11},{11... | collective-permute-start | bytes 27656 | tf_op jit(solution)/shard_map/ppermute | solution.py:28
  (5 other events, 140.5 us)
where the time goes:
time: 264 us; the launch traced here: 263 us
  starting transfers between devices  153 us (58%)
  local copies, waits for them, and re-layouts  44.9 us (17%)
  waiting for transfers between devices  42 us (16%)
  other arithmetic  21.5 us (8%)
    ppermute x12, starting transfers between devices, with_halo(): before = lax.ppermute(last, axis, up)  88.7 us
    ppermute x12, starting transfers between devices, with_halo(): after = lax.ppermute(first, axis, down)  64.6 us
    ppermute x12, waiting for transfers between devices, with_halo(): before = lax.ppermute(last, axis, up)  24.9 us
    ppermute x12, waiting for transfers between devices, with_halo(): after = lax.ppermute(first, axis, down)  17.2 us
    concatenate x6, other arithmetic, with_halo(): x = jnp.concatenate([before, x, after], axis=dim)  11.6 us
    unnamed x29, local copies, waits for them, and re-layouts  9.96 us
    ppermute x2, local copies, waits for them, and re-layouts, with_halo(): before = lax.ppermute(last, axis, up)  8.49 us
    ppermute x2, local copies, waits for them, and re-layouts, with_halo(): after = lax.ppermute(first, axis, down)  7.43 us
  transfers between devices with their start and end apart: 24, of which 9 were waited for; matrix products, arithmetic and copies ran while one was open for 19% of the time, Pallas kernels for 0%

commit v1 on v0

v1 whole, which is shorter than its diff:
```python
import math

import jax
import jax.numpy as jnp
from jax import lax
from jax.experimental import pallas as pl
from jax.experimental.pallas import tpu as pltpu
from jax.sharding import PartitionSpec as P

SWEEPS = 3
NSPEC, NZ, RX, LY = 8, 16, 16, 128
EX = RX + 8
FIELDS = 5
TINY = 1e-30

ZONE_RATES = (0.02, 0.05, 0.1, 0.2)
ZONE_PERMEABILITY = (5.0, 10.0, 20.0, 40.0)
SOLUBILITY = 0.5
MOLAR_VOLUME = 0.05
STORAGE_COEF = 0.2
TIME_STEP = 0.2
CHEB_SPREAD = 0.92
STOICHIOMETRY = (-1.0, -1.0, 0.0, 0.0, 0.0, 0.0, 0.0, 0.0)

F32 = jnp.float32
MESH = pl.DeviceIdType.MESH
DIRS = ((-1, 0), (1, 0), (0, -1), (0, 1), (-1, -1), (1, -1), (-1, 1), (1, 1))
OPPOSITE = tuple(DIRS.index((-a, -b)) for a, b in DIRS)


def relax_weight(iteration):
    return 1.0 / (1.0 + CHEB_SPREAD * math.cos(math.pi * (2 * iteration + 1) / (2 * SWEEPS)))


def lookup(labels, table):
    out = jnp.where(labels == 0, F32(table[0]), F32(table[1]))
    out = jnp.where(labels == 2, F32(table[2]), out)
    return jnp.where(labels == 3, F32(table[3]), out)


def inverse(x):
    guess = pl.reciprocal(x, approx=True)
    guess = guess * (2.0 - x * guess)
    return guess * (2.0 - x * guess)


def harmonic(a, b):
    return (2.0 * a * b) * inverse(jnp.maximum(a + b, TINY))


def lanes(x, shift):
    return pltpu.roll(x, shift % LY if isinstance(shift, int) else lax.rem(shift + 2 * LY, LY), 1)


def before(x):
    return pltpu.roll(x, 1, 0)


def after(x):
    return pltpu.roll(x, x.shape[0] - 1, 0)


def iota(rows, dim):
    return lax.broadcasted_iota(jnp.int32, (rows, LY), dim)


def flow_kernel(sizes, sp_in, por_in, old_in, src_in, zone_in, fix_in,
                sp, phi, rea, pa, tx, tyl, tyr, tz, edge, side, row_lo, row_hi,
                por, zone, fix, pb, perm, stor, rhs, gain,
                sx, sy, sc, ssx, ssy, rx, ry, rc, rsx, rsy,
                in_sem, send_sem, recv_sem, s_send, s_recv):
    gx, gy = lax.axis_index("gx"), lax.axis_index("gy")
    spots = []
    for dx, dy in DIRS:
        there = None
        for here, step, size in ((gx, dx, sizes[0]), (gy, dy, sizes[1])):
            if step:
                ok = here > 0 if step < 0 else here < size - 1
                there = ok if there is None else there & ok
        spots.append(((gx + dx, gy + dy), there))

    barrier = pltpu.get_barrier_semaphore()
    for where, there in spots:
        @pl.when(there)
        def _():
            pl.semaphore_signal(barrier, inc=1, device_id=where, device_id_type=MESH)

    loads = [
        pltpu.make_async_copy(sp_in.at[pl.ds(0, 2)], sp.at[pl.ds(0, 2)], in_sem.at[0]),
        pltpu.make_async_copy(por_in, por, in_sem.at[1]),
        pltpu.make_async_copy(zone_in, zone, in_sem.at[2]),
        pltpu.make_async_copy(old_in, pa.at[pl.ds(1, NZ), pl.ds(0, RX)], in_sem.at[3]),
        pltpu.make_async_copy(src_in, rhs.at[:, pl.ds(0, RX)], in_sem.at[4]),
        pltpu.make_async_copy(fix_in, fix, in_sem.at[5]),
        pltpu.make_async_copy(sp_in.at[pl.ds(2, NSPEC - 2)], sp.at[pl.ds(2, NSPEC - 2)], in_sem.at[6]),
    ]
    for c in loads:
        c.start()

    for i in range(8):
        @pl.when(jnp.logical_not(spots[i][1]))
        def _():
            if i < 2:
                rx[i] = jnp.zeros(rx.shape[1:], F32)
                rsx[i] = jnp.zeros(rsx.shape[1:], F32)
            elif i < 4:
                ry[i - 2] = jnp.zeros(ry.shape[1:], F32)
                rsy[i - 2] = jnp.zeros(rsy.shape[1:], F32)
            else:
                rc[i - 4] = jnp.zeros(rc.shape[1:], F32)
    plane = jnp.zeros((EX, LY), F32)
    for ref in (perm, pa, pb):
        ref[0] = plane
        ref[NZ + 1] = plane

    lane = iota(RX, 1)
    group = lax.shift_right_logical(lane, 3)
    low = (lane & 7) < 4
    for c in loads[:6]:
        c.wait()

    def own(z, packs):
        c0, c1 = sp[0, z], sp[1, z]
        label = zone[z]
        reaction = lookup(label, ZONE_RATES) * (c0 * c1 - SOLUBILITY)
        new = por[z] - MOLAR_VOLUME * reaction
        solid = 1.0 - new
        k = lookup(label, ZONE_PERMEABILITY) * (new * new * new) * inverse(solid * solid)
        s = STORAGE_COEF * new
        free = 1.0 - fix[z].astype(F32)
        p, q = pa[z + 1, :RX], rhs[z, :RX]
        rea[z] = reaction
        phi[z] = new
        perm[z + 1, :RX] = k
        stor[z, :RX] = s
        gain[z, :RX] = free
        out = []
        for f, (v, pack) in enumerate(zip((k, p, s, q, free), packs)):
            sx[0, f, z] = v[:4]
            sx[1, f, z] = v[12:]
            out.append(jnp.where(group == z, lanes(v, 8 * z + 4), pack))
        return tuple(out)

    zero = jnp.zeros((RX, LY), F32)
    packs = lax.fori_loop(0, NZ, own, (zero,) * FIELDS, unroll=2)
    for j in range(3):
        a, b = packs[2 * j], packs[2 * j + 1] if j < 2 else zero
        down = jnp.where(low, lanes(a, -4), b)
        up = jnp.where(low, a, lanes(b, 4))
        sy[0, j] = down
        sy[1, j] = up
        sc[0, j], sc[1, j] = down[:4], down[12:]
        sc[2, j], sc[3, j] = up[:4], up[12:]

    def parts(i):
        if i < 2:
            return sx.at[i], rx, i
        if i < 4:
            return sy.at[i - 2], ry, i - 2
        return sc.at[i - 4], rc, i - 4

    def copy(i):
        src, _, _ = parts(i)
        _, dst, at = parts(OPPOSITE[i])
        return pltpu.make_async_remote_copy(
            src_ref=src, dst_ref=dst.at[at], send_sem=send_sem.at[i],
            recv_sem=recv_sem.at[OPPOSITE[i]], device_id=spots[i][0], device_id_type=MESH)

    def arrival(i):
        src, dst, at = parts(i)
        return pltpu.make_async_remote_copy(
            src_ref=src, dst_ref=dst.at[at], send_sem=send_sem.at[i],
            recv_sem=recv_sem.at[i], device_id=spots[i][0], device_id_type=MESH)

    def sparts(i):
        return (ssx.at[i], rsx, i) if i < 2 else (ssy.at[i - 2], rsy, i - 2)

    def scopy(i):
        src, _, _ = sparts(i)
        _, dst, at = sparts(OPPOSITE[i])
        return pltpu.make_async_remote_copy(
            src_ref=src, dst_ref=dst.at[at], send_sem=s_send.at[i],
            recv_sem=s_recv.at[OPPOSITE[i]], device_id=spots[i][0], device_id_type=MESH)

    def sarrival(i):
        src, dst, at = sparts(i)
        return pltpu.make_async_remote_copy(
            src_ref=src, dst_ref=dst.at[at], send_sem=s_send.at[i],
            recv_sem=s_recv.at[i], device_id=spots[i][0], device_id_type=MESH)

    pl.semaphore_wait(barrier, sum(there.astype(jnp.int32) for _, there in spots))
    for i in (2, 3, 4, 5, 6, 7, 0, 1):
        @pl.when(spots[i][1])
        def _():
            copy(i).start()

    loads[6].wait()
    for s in range(NSPEC):
        for z in range(NZ):
            ssx[0, s, pl.ds(z, 1)] = sp[s, z, pl.ds(0, 1)]
            ssx[1, s, pl.ds(z, 1)] = sp[s, z, pl.ds(RX - 1, 1)]
    pair = lax.shift_right_logical(lane, 1)
    odd = (lane & 1) == 1

    def species_edge(z, packs):
        lo, hi = packs
        for s in range(NSPEC):
            m = lax.rem(z, 8) * 8 + s
            turned = lanes(sp[s, z], 2 * m + 1)
            lo = jnp.where((pair == m) & (z < 8), turned, lo)
            hi = jnp.where((pair == m) & (z >= 8), turned, hi)
        return lo, hi

    lo, hi = lax.fori_loop(0, NZ, species_edge, (zero, zero))
    ssy[0] = jnp.where(odd, lo, lanes(hi, -1))
    ssy[1] = jnp.where(odd, lanes(hi, 1), lo)
    for i in (2, 3, 0, 1):
        @pl.when(spots[i][1])
        def _():
            scopy(i).start()

    for i in range(8):
        @pl.when(spots[i][1])
        def _():
            arrival(i).wait_recv()

    lane8, lane24 = iota(8, 1), iota(EX, 1)
    group8 = lax.shift_right_logical(lane8, 3)
    low24 = (lane24 & 7) < 4

    def rows(z, packs):
        out = []
        for f, pack in enumerate(packs):
            tail = jnp.concatenate([rx[1, f, z], rx[0, f, z]], axis=0)
            if f == 0:
                perm[z + 1, RX:] = tail
            elif f == 1:
                pa[z + 1, RX:] = tail
            else:
                (stor, rhs, gain)[f - 2][z, RX:] = tail
            out.append(jnp.where(group8 == z, lanes(tail, 8 * z + 4), pack))
        return tuple(out)

    tails = lax.fori_loop(0, NZ, rows, (jnp.zeros((8, LY), F32),) * FIELDS, unroll=2)
    whole = [jnp.concatenate([a, b], axis=0) for a, b in zip(packs, tails)]

    strips = []
    for d in range(2):
        fields = []
        for f in range(FIELDS):
            j = f // 2
            halo = jnp.concatenate([ry[d, j], rc[2 * d + 1, j], rc[2 * d, j]], axis=0)
            if d == 0:
                fields.append(jnp.where(low24, halo if f % 2 == 0 else lanes(halo, -4), whole[f]))
            else:
                fields.append(jnp.where(low24, whole[f], lanes(halo, 4) if f % 2 == 0 else halo))
        k, p, s, q, free = fields
        fx_t = harmonic(k, before(k))
        fy_t = harmonic(k, lanes(k, 1))
        fz_t = jnp.where(lane24 < 8, 0.0, harmonic(k, lanes(k, 8)))
        total = s + fx_t + after(fx_t) + fy_t + lanes(fy_t, -1) + fz_t + lanes(fz_t, -8)
        g = free * inverse(jnp.maximum(total, TINY))
        right = s * p + q
        history = [p]
        for it in range(SWEEPS):
            fx = fx_t * (p - before(p))
            fy = fy_t * (p - lanes(p, 1))
            fz = fz_t * (p - lanes(p, 8))
            r = right - s * p - fx + after(fx) - fy + lanes(fy, -1) - fz + lanes(fz, -8)
            p = p + F32(relax_weight(it)) * g * r
            history.append(p)
        strips.append((fy_t, history))
    column = lane24 & 7
    faces = jnp.where(column == 4, strips[0][0], lanes(strips[1][0], -1))
    edges = [jnp.where(column == 3, a, lanes(b, -2)) for a, b in zip(strips[0][1], strips[1][1])]
    edge[...] = edges[SWEEPS][:RX]

    first, last = lane24 == 0, lane24 == LY - 1

    def coefficients(z, tz_lo):
        k = perm[z + 1]
        tz_hi = harmonic(k, perm[z + 2])
        turned = lanes(faces, -(8 * z + 4))
        t_x = harmonic(k, before(k))
        t_lo = jnp.where(first, turned, harmonic(k, lanes(k, 1)))
        t_hi = jnp.where(last, turned, lanes(t_lo, -1))
        s = stor[z]
        total = s + t_x + after(t_x) + t_lo + t_hi + tz_lo + tz_hi
        tx[z], tyl[z], tyr[z], tz[z] = t_x, t_lo, t_hi, tz_lo
        gain[z] = gain[z] * inverse(jnp.maximum(total, TINY))
        rhs[z] = s * pa[z + 1] + rhs[z]
        return tz_hi

    tz[NZ] = lax.fori_loop(0, NZ, coefficients, plane)

    for it in range(SWEEPS):
        src, dst = (pa, pb) if it % 2 == 0 else (pb, pa)

        def sweep(z, flow_lo):
            p = src[z + 1]
            turned = lanes(edges[it], -(8 * z + 3))
            fx = tx[z] * (p - before(p))
            f_lo = tyl[z] * (p - jnp.where(first, turned, lanes(p, 1)))
            f_hi = tyr[z] * (jnp.where(last, turned, lanes(p, -1)) - p)
            flow_hi = tz[z + 1] * (src[z + 2] - p)
            r = rhs[z] - stor[z] * p - fx + after(fx) - f_lo + f_hi - flow_lo + flow_hi
            dst[z + 1] = p + F32(relax_weight(it)) * gain[z] * r
            return flow_hi

        lax.fori_loop(0, NZ, sweep, plane)
    if SWEEPS % 2:
        def back(z, c):
            pa[z + 1] = pb[z + 1]
            return c
        lax.fori_loop(0, NZ, back, 0)

    for i in range(4):
        @pl.when(spots[i][1])
        def _():
            sarrival(i).wait_recv()
    m_lo, m_hi = rsy[0], rsy[1]
    side[0] = jnp.where(odd, lanes(m_lo, 1), lanes(m_hi, -1))
    side[1] = jnp.where(odd, m_lo, m_hi)
    row_lo[...] = rsx[0]
    row_hi[...] = rsx[1]
    for i in range(8):
        @pl.when(spots[i][1])
        def _():
            copy(i).wait_send()
            if i < 4:
                scopy(i).wait_send()


def transport_kernel(sp, phi, rea, p_ref, tx, tyl, tyr, tz, edge, side, row_lo, row_hi,
                     conc_out, p_out, phi_out, conc, sem):
    outs = [
        pltpu.make_async_copy(p_ref.at[pl.ds(1, NZ), pl.ds(0, RX)], p_out, sem.at[0]),
        pltpu.make_async_copy(phi, phi_out, sem.at[1]),
    ]
    for c in outs:
        c.start()
    lane, row = iota(RX, 1), iota(RX, 0)
    first, last = lane == 0, lane == LY - 1
    top, bottom = row == 0, row == RX - 1

    def body(z, carry):
        wide = p_ref[z + 1]
        p = wide[:RX]
        turned = lanes(edge[...], -(8 * z + 3))
        t_x = tx[z]
        flows = [
            t_x[:RX] * (p - before(wide)[:RX]),
            after(t_x)[:RX] * (p - after(wide)[:RX]),
            tyl[z, :RX] * (p - jnp.where(first, turned, lanes(p, 1))),
            tyr[z, :RX] * (p - jnp.where(last, turned, lanes(p, -1))),
            tz[z, :RX] * (p - p_ref[z, :RX]),
            tz[z + 1, :RX] * (p - p_ref[z + 2, :RX]),
        ]
        scale = TIME_STEP * inverse(phi[z])
        out = jnp.maximum(flows[0], 0.0)
        for f in flows[1:]:
            out = out + jnp.maximum(f, 0.0)
        keep = 1.0 - scale * out
        take = [-scale * jnp.minimum(f, 0.0) for f in flows]
        reaction = rea[z]
        z_lo, z_hi = jnp.maximum(z - 1, 0), jnp.minimum(z + 1, NZ - 1)
        half = side[lax.div(z, 8)]
        for s in range(NSPEC):
            c = sp[s, z]
            turned_c = lanes(half, -(2 * (lax.rem(z, 8) * 8 + s) + 1))
            total = c * keep
            total = total + take[0] * jnp.where(top, row_lo[s, pl.ds(z, 1)], before(c))
            total = total + take[1] * jnp.where(bottom, row_hi[s, pl.ds(z, 1)], after(c))
            total = total + take[2] * jnp.where(first, turned_c, lanes(c, 1))
            total = total + take[3] * jnp.where(last, turned_c, lanes(c, -1))
            total = total + take[4] * sp[s, z_lo]
            total = total + take[5] * sp[s, z_hi]
            if STOICHIOMETRY[s]:
                total = total + STOICHIOMETRY[s] * reaction
            conc[s, z] = total
        return carry

    for part in range(4):
        lax.fori_loop(4 * part, 4 * part + 4, body, 0)
        at = pl.ds(4 * part, 4)
        c = pltpu.make_async_copy(conc.at[:, at], conc_out.at[:, at], sem.at[2 + part])
        c.start()
        outs.append(c)
    for c in outs:
        c.wait()


def build(sizes):
    tile = (NZ, RX, LY)
    wide = (NZ, EX, LY)
    species = (NSPEC, NZ, RX, LY)
    vmem = pl.BlockSpec(memory_space=pltpu.VMEM)
    hbm = pl.BlockSpec(memory_space=pltpu.HBM)

    def shards(sp, por, old, src, zone, fix):
        middle = [
            species, tile, tile, (NZ + 2, EX, LY), wide, wide, wide, (NZ + 1, EX, LY),
            (RX, LY), (2, RX, LY), (NSPEC, NZ, LY), (NSPEC, NZ, LY),
        ]
        shared = pl.pallas_call(
            lambda *refs: flow_kernel(sizes, *refs),
            out_shape=[pltpu.VMEM(shape, F32) for shape in middle],
            in_specs=[hbm] * 6,
            out_specs=[vmem] * len(middle),
            scratch_shapes=[
                pltpu.VMEM(tile, F32), pltpu.VMEM(tile, jnp.int32), pltpu.VMEM(tile, jnp.int32),
                pltpu.VMEM((NZ + 2, EX, LY), F32), pltpu.VMEM((NZ + 2, EX, LY), F32),
                pltpu.VMEM(wide, F32), pltpu.VMEM(wide, F32), pltpu.VMEM(wide, F32),
                pltpu.VMEM((2, FIELDS, NZ, 4, LY), F32), pltpu.VMEM((2, 3, RX, LY), F32),
                pltpu.VMEM((4, 3, 4, LY), F32), pltpu.VMEM((2, NSPEC, NZ, LY), F32),
                pltpu.VMEM((2, RX, LY), F32),
                pltpu.VMEM((2, FIELDS, NZ, 4, LY), F32), pltpu.VMEM((2, 3, RX, LY), F32),
                pltpu.VMEM((4, 3, 4, LY), F32), pltpu.VMEM((2, NSPEC, NZ, LY), F32),
                pltpu.VMEM((2, RX, LY), F32),
                pltpu.SemaphoreType.DMA((7,)), pltpu.SemaphoreType.DMA((8,)),
                pltpu.SemaphoreType.DMA((8,)), pltpu.SemaphoreType.DMA((4,)),
                pltpu.SemaphoreType.DMA((4,)),
            ],
            compiler_params=pltpu.CompilerParams(
                collective_id=0, has_side_effects=True, vmem_limit_bytes=32 * 2**20),
            name="flow",
        )(sp, por, old, src, zone, fix)
        return tuple(pl.pallas_call(
            transport_kernel,
            out_shape=[jax.ShapeDtypeStruct(s, F32) for s in (species, tile, tile)],
            in_specs=[vmem] * len(middle),
            out_specs=[hbm] * 3,
            scratch_shapes=[pltpu.VMEM(species, F32), pltpu.SemaphoreType.DMA((6,))],
            compiler_params=pltpu.CompilerParams(vmem_limit_bytes=16 * 2**20),
            name="transport",
        )(*shared))

    return shards


def solution(mesh):
    specs = (P(None, None, "gx", "gy"),) + (P(None, "gx", "gy"),) * 5
    outs = (P(None, None, "gx", "gy"), P(None, "gx", "gy"), P(None, "gx", "gy"))
    sizes = (mesh.shape["gx"], mesh.shape["gy"])
    return jax.shard_map(build(sizes), mesh=mesh, in_specs=specs, out_specs=outs, check_vma=False)
```

time: 264 us -> 42 us (0.16)
  the two profiles are of different devices: /device:TPU:30 before, /device:TPU:29 now
where the time goes in v1:
time: 42 us; the launch traced here: 41.8 us
  Pallas kernels  35.4 us (84%)
  local copies, waits for them, and re-layouts  5.74 us (14%)
  between operations  0.65 us (2%)
    pallas_call x1, Pallas kernels, shards(): pl.pallas_call(lambda *refs: flow_kernel(sizes, *refs), out_shape=[pltpu....  32.4 us
    unnamed x12, local copies, waits for them, and re-layouts  5.74 us
    pallas_call x1, Pallas kernels, shards(): pl.pallas_call(transport_kernel, out_shape=[jax.ShapeDtypeStruct(s, F32)...  2.95 us

profile of v1, /device:TPU:29, one launch (start us, length us, event | category | flops | bytes accessed | tf_op | source)
XLA Modules:
  0.0 41.8 jit_solution(16226508548031305359)
XLA Ops:
  0.6 0.0 copy-start
  0.6 1.2 %copy-done = f32[8,16,16,128]{3,2,1,0:T(8,128)S(1)} copy-done((f32[8,16,16,128]{3,2,1,0:T(8,128)S(1)}, f32[8,16,16,128]{3,2,1,0:T(8,128)}, u32[]{:S(2)}) %copy-start) | copy-done | bytes 1048600
  1.9 0.0 copy-start.1
  1.9 0.9 %copy-done.1 = f32[16,16,128]{2,1,0:T(8,128)S(1)} copy-done((f32[16,16,128]{2,1,0:T(8,128)S(1)}, f32[16,16,128]{2,1,0:T(8,128)}, u32[]{:S(2)}) %copy-start.1) | copy-done | bytes 131096
  2.8 0.0 copy-start.2
  2.8 0.9 %copy-done.2 = f32[16,16,128]{2,1,0:T(8,128)S(1)} copy-done((f32[16,16,128]{2,1,0:T(8,128)S(1)}, f32[16,16,128]{2,1,0:T(8,128)}, u32[]{:S(2)}) %copy-start.2) | copy-done | bytes 131096
  3.7 0.0 copy-start.3
  3.7 0.9 %copy-done.3 = f32[16,16,128]{2,1,0:T(8,128)S(1)} copy-done((f32[16,16,128]{2,1,0:T(8,128)S(1)}, f32[16,16,128]{2,1,0:T(8,128)}, u32[]{:S(2)}) %copy-start.3) | copy-done | bytes 131096
  4.6 0.0 copy-start.4
  4.6 0.9 %copy-done.4 = s32[16,16,128]{2,1,0:T(8,128)S(1)} copy-done((s32[16,16,128]{2,1,0:T(8,128)S(1)}, s32[16,16,128]{2,1,0:T(8,128)}, u32[]{:S(2)}) %copy-start.4) | copy-done | bytes 131096
  5.5 0.0 copy-start.5
  5.5 0.9 %copy-done.5 = s32[16,16,128]{2,1,0:T(8,128)S(1)} copy-done((s32[16,16,128]{2,1,0:T(8,128)S(1)}, s32[16,16,128]{2,1,0:T(8,128)}, u32[]{:S(2)}) %copy-start.5) | copy-done | bytes 131096
  6.4 32.4 %flow.1 = (f32[8,16,16,128]{3,2,1,0:T(8,128)S(1)}, f32[16,16,128]{2,1,0:T(8,128)S(1)}, f32[16,16,128]{2,1,0:T(8,128)S(1)}, f32[18,24,128]{2,1,0:T(8,128)S(1)}, f...) custom-call(f32[8,16,16,128]{3,2,1,0:T(8,128)S(1)} %copy-done, ...), custom_call_target="tpu_custom_call" | custom-call | tf_op jit(solution)/shard_map/flow/pallas_call | solution.py:405
  38.8 3.0 %transport.1 = (f32[8,16,16,128]{3,2,1,0:T(8,128)}, f32[16,16,128]{2,1,0:T(8,128)}, f32[16,16,128]{2,1,0:T(8,128)}) custom-call(f32[8,16,16,128]{3,2,1,0:T(8,128)S(1)} %get-tuple-element.15.sp, f32[16,16,128]{2,1,0:T(8,128)S(1)} %get-tuple-element.16.phi, f32[16,16,128]{2,1,0:T(8,128)S(1)} %get-tuple-element.17.rea, ...), custom_call_target="tpu_custom_call" | custom-call | tf_op jit(solution)/shard_map/transport/pallas_call | solution.py:428
Async XLA Ops:
  0.6 1.2 %copy-start = (f32[8,16,16,128]{3,2,1,0:T(8,128)S(1)}, f32[8,16,16,128]{3,2,1,0:T(8,128)}, u32[]{:S(2)}) copy-start(f32[8,16,16,128]{3,2,1,0:T(8,128)} %refs_0_.1) | copy-start | bytes 3145732
  1.9 0.9 %copy-start.1 = (f32[16,16,128]{2,1,0:T(8,128)S(1)}, f32[16,16,128]{2,1,0:T(8,128)}, u32[]{:S(2)}) copy-start(f32[16,16,128]{2,1,0:T(8,128)} %refs_1_.1) | copy-start | bytes 393220
  2.8 0.9 %copy-start.2 = (f32[16,16,128]{2,1,0:T(8,128)S(1)}, f32[16,16,128]{2,1,0:T(8,128)}, u32[]{:S(2)}) copy-start(f32[16,16,128]{2,1,0:T(8,128)} %refs_2_.1) | copy-start | bytes 393220
  3.7 0.9 %copy-start.3 = (f32[16,16,128]{2,1,0:T(8,128)S(1)}, f32[16,16,128]{2,1,0:T(8,128)}, u32[]{:S(2)}) copy-start(f32[16,16,128]{2,1,0:T(8,128)} %refs_3_.1) | copy-start | bytes 393220
  4.6 0.9 %copy-start.4 = (s32[16,16,128]{2,1,0:T(8,128)S(1)}, s32[16,16,128]{2,1,0:T(8,128)}, u32[]{:S(2)}) copy-start(s32[16,16,128]{2,1,0:T(8,128)} %refs_4_.1) | copy-start | bytes 393220
  5.5 0.9 %copy-start.5 = (s32[16,16,128]{2,1,0:T(8,128)S(1)}, s32[16,16,128]{2,1,0:T(8,128)}, u32[]{:S(2)}) copy-start(s32[16,16,128]{2,1,0:T(8,128)} %refs_5_.1) | copy-start | bytes 393220

commit v2 on v1

--- a/solution.py
+++ b/solution.py
@@ -65,8 +65,8 @@
 
 
 def flow_kernel(sizes, sp_in, por_in, old_in, src_in, zone_in, fix_in,
-                sp, phi, rea, pa, tx, tyl, tyr, tz, edge, side, row_lo, row_hi,
-                por, zone, fix, pb, perm, stor, rhs, gain,
+                sp, phi, rea, pb, tx, tyl, tyr, tz, edge, side, row_lo, row_hi,
+                por, zone, fix, pa, perm, stor, rhs, gain,
                 sx, sy, sc, ssx, ssy, rx, ry, rc, rsx, rsy,
                 in_sem, send_sem, recv_sem, s_send, s_recv):
     gx, gy = lax.axis_index("gx"), lax.axis_index("gy")
@@ -142,7 +142,7 @@
         return tuple(out)
 
     zero = jnp.zeros((RX, LY), F32)
-    packs = lax.fori_loop(0, NZ, own, (zero,) * FIELDS, unroll=2)
+    packs = lax.fori_loop(0, NZ, own, (zero,) * FIELDS, unroll=8)
     for j in range(3):
         a, b = packs[2 * j], packs[2 * j + 1] if j < 2 else zero
         down = jnp.where(low, lanes(a, -4), b)
@@ -211,7 +211,7 @@
             hi = jnp.where((pair == m) & (z >= 8), turned, hi)
         return lo, hi
 
-    lo, hi = lax.fori_loop(0, NZ, species_edge, (zero, zero))
+    lo, hi = lax.fori_loop(0, NZ, species_edge, (zero, zero), unroll=2)
     ssy[0] = jnp.where(odd, lo, lanes(hi, -1))
     ssy[1] = jnp.where(odd, lanes(hi, 1), lo)
     for i in (2, 3, 0, 1):
@@ -241,7 +241,7 @@
             out.append(jnp.where(group8 == z, lanes(tail, 8 * z + 4), pack))
         return tuple(out)
 
-    tails = lax.fori_loop(0, NZ, rows, (jnp.zeros((8, LY), F32),) * FIELDS, unroll=2)
+    tails = lax.fori_loop(0, NZ, rows, (jnp.zeros((8, LY), F32),) * FIELDS, unroll=8)
     whole = [jnp.concatenate([a, b], axis=0) for a, b in zip(packs, tails)]
 
     strips = []
@@ -291,7 +291,7 @@
         rhs[z] = s * pa[z + 1] + rhs[z]
         return tz_hi
 
-    tz[NZ] = lax.fori_loop(0, NZ, coefficients, plane)
+    tz[NZ] = lax.fori_loop(0, NZ, coefficients, plane, unroll=NZ)
 
     for it in range(SWEEPS):
         src, dst = (pa, pb) if it % 2 == 0 else (pb, pa)
@@ -307,12 +307,7 @@
             dst[z + 1] = p + F32(relax_weight(it)) * gain[z] * r
             return flow_hi
 
-        lax.fori_loop(0, NZ, sweep, plane)
-    if SWEEPS % 2:
-        def back(z, c):
-            pa[z + 1] = pb[z + 1]
-            return c
-        lax.fori_loop(0, NZ, back, 0)
+        lax.fori_loop(0, NZ, sweep, plane, unroll=NZ)
 
     for i in range(4):
         @pl.when(spots[i][1])
@@ -381,7 +376,7 @@
         return carry
 
     for part in range(4):
-        lax.fori_loop(4 * part, 4 * part + 4, body, 0)
+        lax.fori_loop(4 * part, 4 * part + 4, body, 0, unroll=4)
         at = pl.ds(4 * part, 4)
         c = pltpu.make_async_copy(conc.at[:, at], conc_out.at[:, at], sem.at[2 + part])
         c.start()
@@ -397,7 +392,8 @@
     vmem = pl.BlockSpec(memory_space=pltpu.VMEM)
     hbm = pl.BlockSpec(memory_space=pltpu.HBM)
 
-    def shards(sp, por, old, src, zone, fix):
+    def shards(*args):
+        args = [pltpu.with_memory_space_constraint(a, pltpu.HBM) for a in args]
         middle = [
             species, tile, tile, (NZ + 2, EX, LY), wide, wide, wide, (NZ + 1, EX, LY),
             (RX, LY), (2, RX, LY), (NSPEC, NZ, LY), (NSPEC, NZ, LY),
@@ -424,7 +420,7 @@
             compiler_params=pltpu.CompilerParams(
                 collective_id=0, has_side_effects=True, vmem_limit_bytes=32 * 2**20),
             name="flow",
-        )(sp, por, old, src, zone, fix)
+        )(*args)
         return tuple(pl.pallas_call(
             transport_kernel,
             out_shape=[jax.ShapeDtypeStruct(s, F32) for s in (species, tile, tile)],

time: 42 us -> 28.3 us (0.67)
  Pallas kernels: 35.4 us -> 27.6 us
  local copies, waits for them, and re-layouts: 5.74 us -> 0 us
    pallas_call x1, Pallas kernels: 32.4 us -> 25.7 us  [shards(): pl.pallas_call(lambda *refs: flow_kernel(sizes, *refs), out_shape=[pltpu....]
    unnamed x12 -> x0, local copies, waits for them, and re-layouts: 5.74 us -> none
    pallas_call x1, Pallas kernels: 2.95 us -> 1.88 us  [shards(): pl.pallas_call(transport_kernel, out_shape=[jax.ShapeDtypeStruct(s, F32)...]
where the time goes in v2:
time: 28.3 us; the launch traced here: 28.2 us
  Pallas kernels  27.6 us (98%)
  between operations  0.64 us (2%)
    pallas_call x1, Pallas kernels, shards(): pl.pallas_call(lambda *refs: flow_kernel(sizes, *refs), out_shape=[pltpu....  25.7 us
    pallas_call x1, Pallas kernels, shards(): pl.pallas_call(transport_kernel, out_shape=[jax.ShapeDtypeStruct(s, F32)...  1.88 us

profile of v2, /device:TPU:29, one launch (start us, length us, event | category | flops | bytes accessed | tf_op | source)
XLA Modules:
  0.0 28.2 jit_solution(4502826841837049521)
XLA Ops:
  0.6 25.7 %flow.1 = (f32[8,16,16,128]{3,2,1,0:T(8,128)S(1)}, f32[16,16,128]{2,1,0:T(8,128)S(1)}, f32[16,16,128]{2,1,0:T(8,128)S(1)}, f32[18,24,128]{2,1,0:T(8,128)S(1)}, f...) custom-call(f32[8,16,16,128]{3,2,1,0:T(8,128)} %refs_0_.1, ...), custom_call_target="tpu_custom_call" | custom-call | tf_op jit(solution)/shard_map/flow/pallas_call | solution.py:401
  26.3 1.9 %transport.1 = (f32[8,16,16,128]{3,2,1,0:T(8,128)}, f32[16,16,128]{2,1,0:T(8,128)}, f32[16,16,128]{2,1,0:T(8,128)}) custom-call(f32[8,16,16,128]{3,2,1,0:T(8,128)S(1)} %get-tuple-element.15.sp, f32[16,16,128]{2,1,0:T(8,128)S(1)} %get-tuple-element.16.phi, f32[16,16,128]{2,1,0:T(8,128)S(1)} %get-tuple-element.17.rea, ...), custom_call_target="tpu_custom_call" | custom-call | tf_op jit(solution)/shard_map/transport/pallas_call | solution.py:424

commit v3 on v2

--- a/solution.py
+++ b/solution.py
@@ -68,7 +68,7 @@
                 sp, phi, rea, pb, tx, tyl, tyr, tz, edge, side, row_lo, row_hi,
                 por, zone, fix, pa, perm, stor, rhs, gain,
                 sx, sy, sc, ssx, ssy, rx, ry, rc, rsx, rsy,
-                in_sem, send_sem, recv_sem, s_send, s_recv):
+                in_sem, send_sem, recv_sem, s_send, s_recv, ready):
     gx, gy = lax.axis_index("gx"), lax.axis_index("gy")
     spots = []
     for dx, dy in DIRS:
@@ -79,11 +79,21 @@
                 there = ok if there is None else there & ok
         spots.append(((gx + dx, gy + dy), there))
 
+    seam = sizes[1] // 2
+    split = jnp.bool_(sizes[1] >= 4)
+    at_lo, at_hi = (gy == seam - 1) & split, (gy == seam) & split
+    at_seam = at_lo | at_hi
     barrier = pltpu.get_barrier_semaphore()
-    for where, there in spots:
-        @pl.when(there)
+    expected = 0
+    for i, (where, there) in enumerate(spots):
+        far = (at_lo & (DIRS[i][1] > 0)) | (at_hi & (DIRS[i][1] < 0))
+        counts = split & ((where[1] == seam - 1) | (where[1] == seam))
+        beside = there & (far | jnp.logical_not(counts))
+
+        @pl.when(beside)
         def _():
             pl.semaphore_signal(barrier, inc=1, device_id=where, device_id_type=MESH)
+        expected = expected + (there & (far | jnp.logical_not(at_seam))).astype(jnp.int32)
 
     loads = [
         pltpu.make_async_copy(sp_in.at[pl.ds(0, 2)], sp.at[pl.ds(0, 2)], in_sem.at[0]),
@@ -188,11 +198,33 @@
             src_ref=src, dst_ref=dst.at[at], send_sem=s_send.at[i],
             recv_sem=s_recv.at[i], device_id=spots[i][0], device_id_type=MESH)
 
-    pl.semaphore_wait(barrier, sum(there.astype(jnp.int32) for _, there in spots))
-    for i in (2, 3, 4, 5, 6, 7, 0, 1):
-        @pl.when(spots[i][1])
-        def _():
-            copy(i).start()
+    def send(only, order, make):
+        for i in order:
+            @pl.when(spots[i][1] & only)
+            def _():
+                make(i).start()
+
+    inner = jnp.logical_not(at_seam)
+
+    @pl.when(at_hi)
+    def _():
+        pl.semaphore_wait(barrier, expected)
+    send(at_hi, (2, 4, 5), copy)
+
+    @pl.when(inner)
+    def _():
+        pl.semaphore_wait(barrier, expected)
+    for edge_row, step in ((seam - 2, 1), (seam + 1, -1)):
+        @pl.when((gy == edge_row) & split)
+        def _():
+            pl.semaphore_signal(ready, inc=1, device_id=(gx, gy + step), device_id_type=MESH)
+
+    @pl.when(at_seam)
+    def _():
+        pl.semaphore_wait(ready, 1)
+    send(inner | at_lo, (2, 4, 5), copy)
+    send(inner | at_hi, (3, 6, 7), copy)
+    send(True, (0, 1), copy)
 
     loads[6].wait()
     for s in range(NSPEC):
@@ -214,10 +246,14 @@
     lo, hi = lax.fori_loop(0, NZ, species_edge, (zero, zero), unroll=2)
     ssy[0] = jnp.where(odd, lo, lanes(hi, -1))
     ssy[1] = jnp.where(odd, lanes(hi, 1), lo)
-    for i in (2, 3, 0, 1):
-        @pl.when(spots[i][1])
-        def _():
-            scopy(i).start()
+    send(True, (2, 0, 1), scopy)
+    send(inner | at_hi, (3,), scopy)
+
+    @pl.when(at_lo)
+    def _():
+        pl.semaphore_wait(barrier, expected)
+    send(at_lo, (3, 6, 7), copy)
+    send(at_lo, (3,), scopy)
 
     for i in range(8):
         @pl.when(spots[i][1])
@@ -415,7 +451,7 @@
                 pltpu.VMEM((2, RX, LY), F32),
                 pltpu.SemaphoreType.DMA((7,)), pltpu.SemaphoreType.DMA((8,)),
                 pltpu.SemaphoreType.DMA((8,)), pltpu.SemaphoreType.DMA((4,)),
-                pltpu.SemaphoreType.DMA((4,)),
+                pltpu.SemaphoreType.DMA((4,)), pltpu.SemaphoreType.REGULAR,
             ],
             compiler_params=pltpu.CompilerParams(
                 collective_id=0, has_side_effects=True, vmem_limit_bytes=32 * 2**20),

time: 28.3 us -> 26.9 us (0.951)
  the two profiles are of different devices: /device:TPU:29 before, /device:TPU:30 now
where the time goes in v3:
time: 26.9 us; the launch traced here: 26.7 us
  Pallas kernels  26.1 us (97%)
  between operations  0.64 us (2%)
    pallas_call x1, Pallas kernels, shards(): pl.pallas_call(lambda *refs: flow_kernel(sizes, *refs), out_shape=[pltpu....  24.2 us
    pallas_call x1, Pallas kernels, shards(): pl.pallas_call(transport_kernel, out_shape=[jax.ShapeDtypeStruct(s, F32)...  1.88 us

profile of v3, /device:TPU:30, one launch (start us, length us, event | category | flops | bytes accessed | tf_op | source)
XLA Modules:
  0.0 26.7 jit_solution(10246072582599435606)
XLA Ops:
  0.6 24.2 %flow.1 = (f32[8,16,16,128]{3,2,1,0:T(8,128)S(1)}, f32[16,16,128]{2,1,0:T(8,128)S(1)}, f32[16,16,128]{2,1,0:T(8,128)S(1)}, f32[18,24,128]{2,1,0:T(8,128)S(1)}, f...) custom-call(f32[8,16,16,128]{3,2,1,0:T(8,128)} %refs_0_.1, ...), custom_call_target="tpu_custom_call" | custom-call | tf_op jit(solution)/shard_map/flow/pallas_call | solution.py:437
  24.9 1.9 %transport.1 = (f32[8,16,16,128]{3,2,1,0:T(8,128)}, f32[16,16,128]{2,1,0:T(8,128)}, f32[16,16,128]{2,1,0:T(8,128)}) custom-call(f32[8,16,16,128]{3,2,1,0:T(8,128)S(1)} %get-tuple-element.15.sp, f32[16,16,128]{2,1,0:T(8,128)S(1)} %get-tuple-element.16.phi, f32[16,16,128]{2,1,0:T(8,128)S(1)} %get-tuple-element.17.rea, ...), custom_call_target="tpu_custom_call" | custom-call | tf_op jit(solution)/shard_map/transport/pallas_call | solution.py:460

commit v4 on v3

v4 whole, which is shorter than its diff:
```python
import math

import jax
import jax.numpy as jnp
from jax import lax
from jax.experimental import pallas as pl
from jax.experimental.pallas import tpu as pltpu
from jax.sharding import PartitionSpec as P

SWEEPS = 3
NSPEC, NZ, RX, LY = 8, 16, 16, 128
EX = RX + 8
FIELDS = 5
TINY = 1e-30
PLANES = [(f, d) for f in range(FIELDS) for d in range(4 if f < 2 else 3)]

ZONE_RATES = (0.02, 0.05, 0.1, 0.2)
ZONE_PERMEABILITY = (5.0, 10.0, 20.0, 40.0)
SOLUBILITY = 0.5
MOLAR_VOLUME = 0.05
STORAGE_COEF = 0.2
TIME_STEP = 0.2
CHEB_SPREAD = 0.92
STOICHIOMETRY = (-1.0, -1.0, 0.0, 0.0, 0.0, 0.0, 0.0, 0.0)

F32 = jnp.float32
MESH = pl.DeviceIdType.MESH
DIRS = ((-1, 0), (1, 0), (0, -1), (0, 1), (-1, -1), (1, -1), (-1, 1), (1, 1))
OPPOSITE = tuple(DIRS.index((-a, -b)) for a, b in DIRS)


def relax_weight(iteration):
    return 1.0 / (1.0 + CHEB_SPREAD * math.cos(math.pi * (2 * iteration + 1) / (2 * SWEEPS)))


def lookup(labels, table):
    out = jnp.where(labels == 0, F32(table[0]), F32(table[1]))
    out = jnp.where(labels == 2, F32(table[2]), out)
    return jnp.where(labels == 3, F32(table[3]), out)


def inverse(x):
    guess = pl.reciprocal(x, approx=True)
    guess = guess * (2.0 - x * guess)
    return guess * (2.0 - x * guess)


def harmonic(a, b):
    return (2.0 * a * b) * inverse(jnp.maximum(a + b, TINY))


def lanes(x, shift):
    return pltpu.roll(x, shift % LY if isinstance(shift, int) else lax.rem(shift + 2 * LY, LY), 1)


def before(x):
    return pltpu.roll(x, 1, 0)


def after(x):
    return pltpu.roll(x, x.shape[0] - 1, 0)


def iota(rows, dim):
    return lax.broadcasted_iota(jnp.int32, (rows, LY), dim)


def flow_kernel(sizes, sp_in, por_in, old_in, src_in, zone_in, fix_in,
                sp, phi, rea, pb, tx, ty, tz, face, edge, side, row_lo, row_hi,
                por, zone, fix, old, src, pa, perm, stor, rhs, gain,
                sx, sy, sc, ssx, ssy, rx, ry, rc, rsx, rsy,
                in_sem, send_sem, recv_sem, s_send, s_recv, ready):
    gx, gy = lax.axis_index("gx"), lax.axis_index("gy")
    spots = []
    for dx, dy in DIRS:
        there = None
        for here, step, size in ((gx, dx, sizes[0]), (gy, dy, sizes[1])):
            if step:
                ok = here > 0 if step < 0 else here < size - 1
                there = ok if there is None else there & ok
        spots.append(((gx + dx, gy + dy), there))

    seam = sizes[1] // 2
    split = jnp.bool_(sizes[1] >= 4)
    at_lo, at_hi = (gy == seam - 1) & split, (gy == seam) & split
    at_seam = at_lo | at_hi
    barrier = pltpu.get_barrier_semaphore()
    expected = 0
    for i, (where, there) in enumerate(spots):
        far = (at_lo & (DIRS[i][1] > 0)) | (at_hi & (DIRS[i][1] < 0))
        counts = split & ((where[1] == seam - 1) | (where[1] == seam))
        beside = there & (far | jnp.logical_not(counts))

        @pl.when(beside)
        def _():
            pl.semaphore_signal(barrier, inc=1, device_id=where, device_id_type=MESH)
        expected = expected + (there & (far | jnp.logical_not(at_seam))).astype(jnp.int32)

    loads = [
        pltpu.make_async_copy(sp_in.at[pl.ds(0, 2)], sp.at[pl.ds(0, 2)], in_sem.at[0]),
        pltpu.make_async_copy(zone_in, zone, in_sem.at[1]),
        pltpu.make_async_copy(por_in, por, in_sem.at[2]),
        pltpu.make_async_copy(old_in, old, in_sem.at[3]),
        pltpu.make_async_copy(src_in, src, in_sem.at[4]),
        pltpu.make_async_copy(fix_in, fix, in_sem.at[5]),
        pltpu.make_async_copy(sp_in.at[pl.ds(2, NSPEC - 2)], sp.at[pl.ds(2, NSPEC - 2)], in_sem.at[6]),
    ]
    for c in loads:
        c.start()

    for i in range(8):
        @pl.when(jnp.logical_not(spots[i][1]))
        def _():
            if i < 2:
                rx[i] = jnp.zeros(rx.shape[1:], F32)
                rsx[i] = jnp.zeros(rsx.shape[1:], F32)
            elif i < 4:
                ry[i - 2] = jnp.zeros(ry.shape[1:], F32)
                rsy[i - 2] = jnp.zeros(rsy.shape[1:], F32)
            else:
                rc[i - 4] = jnp.zeros(rc.shape[1:], F32)
    plane = jnp.zeros((EX, LY), F32)
    for ref in (perm, pa, pb):
        ref[pl.ds(0, EX)] = plane
        ref[pl.ds((NZ + 1) * EX, EX)] = plane
    for ref in (stor, rhs, gain):
        for z in range(NZ):
            ref[pl.ds(z * EX + RX, 8)] = plane[:8]

    lane = iota(RX, 1)
    group = lax.shift_right_logical(lane, 3)
    low = (lane & 7) < 4
    for c in loads[:6]:
        c.wait()

    def at(z, rows=EX, skip=0):
        return pl.ds(pl.multiple_of(z * EX + skip, 8), rows)

    def own(z, packs):
        rows = pl.ds(pl.multiple_of(z * RX, 8), RX)
        c0, c1 = sp[0, rows], sp[1, rows]
        label = zone[z]
        reaction = lookup(label, ZONE_RATES) * (c0 * c1 - SOLUBILITY)
        new = por[z] - MOLAR_VOLUME * reaction
        solid = 1.0 - new
        k = lookup(label, ZONE_PERMEABILITY) * (new * new * new) * inverse(solid * solid)
        s = STORAGE_COEF * new
        free = 1.0 - fix[z].astype(F32)
        p, q = old[z], src[z]
        rea[z] = reaction
        phi[z] = new
        perm[at(z + 1, RX)] = k
        pa[at(z + 1, RX)] = p
        stor[at(z, RX)] = s
        rhs[at(z, RX)] = q
        gain[at(z, RX)] = free
        return tuple(jnp.where(group == z, lanes(v, 8 * z + 4), pack) for v, pack in zip((k, p, s, q, free), packs))

    zero = jnp.zeros((RX, LY), F32)
    packs = lax.fori_loop(0, NZ, own, (zero,) * FIELDS, unroll=NZ)
    k, p, s, q, free = packs
    low8 = low[:8]
    for side_y in range(2):
        if side_y == 0:
            a, b = jnp.where(low, lanes(k, -4), p), jnp.where(low, lanes(s, -4), q)
            m = jnp.where(low8, lanes(free[:8], -4), free[8:])
        else:
            a, b = jnp.where(low, k, lanes(p, 4)), jnp.where(low, s, lanes(q, 4))
            m = jnp.where(low8, free[:8], lanes(free[8:], 4))
        sy[side_y, pl.ds(0, RX)] = a
        sy[side_y, pl.ds(RX, RX)] = b
        sy[side_y, pl.ds(2 * RX, 8)] = m
        for side_x in range(2):
            j = 2 * side_y + side_x
            if side_x == 0:
                parts_c = (a[:3], b[:2], free[:2])
            else:
                parts_c = (a[RX - 3:], b[RX - 2:], free[RX - 2:])
            sc[j, pl.ds(0, 3)] = parts_c[0]
            sc[j, pl.ds(3, 2)] = parts_c[1]
            sc[j, pl.ds(5, 2)] = parts_c[2]
            sc[j, pl.ds(7, 1)] = parts_c[2][:1]

    def strided(ref, z0, row):
        return ref.at[pl.ds(z0 * EX + row, NZ, stride=EX)]

    fields = ((perm, 1), (pa, 1), (stor, 0), (rhs, 0), (gain, 0))
    for n, (f, d) in enumerate(PLANES):
        ref, z0 = fields[f]
        sx[0, n] = strided(ref, z0, d)[...]
        sx[1, n] = strided(ref, z0, RX - 1 - d)[...]

    def parts(i):
        if i < 2:
            return sx.at[i], rx, i
        if i < 4:
            return sy.at[i - 2], ry, i - 2
        return sc.at[i - 4], rc, i - 4

    def copy(i):
        from_ref, _, _ = parts(i)
        _, dst, slot = parts(OPPOSITE[i])
        return pltpu.make_async_remote_copy(
            src_ref=from_ref, dst_ref=dst.at[slot], send_sem=send_sem.at[i],
            recv_sem=recv_sem.at[OPPOSITE[i]], device_id=spots[i][0], device_id_type=MESH)

    def arrival(i):
        from_ref, dst, slot = parts(i)
        return pltpu.make_async_remote_copy(
            src_ref=from_ref, dst_ref=dst.at[slot], send_sem=send_sem.at[i],
            recv_sem=recv_sem.at[i], device_id=spots[i][0], device_id_type=MESH)

    def sparts(i):
        return (ssx.at[i], rsx, i) if i < 2 else (ssy.at[i - 2], rsy, i - 2)

    def scopy(i):
        from_ref, _, _ = sparts(i)
        _, dst, slot = sparts(OPPOSITE[i])
        return pltpu.make_async_remote_copy(
            src_ref=from_ref, dst_ref=dst.at[slot], send_sem=s_send.at[i],
            recv_sem=s_recv.at[OPPOSITE[i]], device_id=spots[i][0], device_id_type=MESH)

    def sarrival(i):
        from_ref, dst, slot = sparts(i)
        return pltpu.make_async_remote_copy(
            src_ref=from_ref, dst_ref=dst.at[slot], send_sem=s_send.at[i],
            recv_sem=s_recv.at[i], device_id=spots[i][0], device_id_type=MESH)

    def send(only, order, make):
        for i in order:
            @pl.when(spots[i][1] & only)
            def _():
                make(i).start()

    inner = jnp.logical_not(at_seam)

    @pl.when(at_hi)
    def _():
        pl.semaphore_wait(barrier, expected)
    send(at_hi, (2, 4, 5), copy)

    @pl.when(inner)
    def _():
        pl.semaphore_wait(barrier, expected)
    for edge_row, step in ((seam - 2, 1), (seam + 1, -1)):
        @pl.when((gy == edge_row) & split)
        def _():
            pl.semaphore_signal(ready, inc=1, device_id=(gx, gy + step), device_id_type=MESH)

    @pl.when(at_seam)
    def _():
        pl.semaphore_wait(ready, 1)
    send(True, (0, 1), copy)
    send(inner | at_lo, (2, 4, 5), copy)
    send(inner | at_hi, (3, 6, 7), copy)

    loads[6].wait()
    for s in range(NSPEC):
        ssx[0, s] = sp[s, pl.ds(0, NZ, stride=RX)]
        ssx[1, s] = sp[s, pl.ds(RX - 1, NZ, stride=RX)]
    pair = lax.shift_right_logical(lane, 1)
    odd = (lane & 1) == 1

    def species_edge(z, packs):
        lo, hi = packs
        for s in range(NSPEC):
            m = lax.rem(z, 8) * 8 + s
            turned = lanes(sp[s, pl.ds(pl.multiple_of(z * RX, 8), RX)], 2 * m + 1)
            lo = jnp.where((pair == m) & (z < 8), turned, lo)
            hi = jnp.where((pair == m) & (z >= 8), turned, hi)
        return lo, hi

    lo, hi = lax.fori_loop(0, NZ, species_edge, (zero, zero), unroll=2)
    ssy[0] = jnp.where(odd, lo, lanes(hi, -1))
    ssy[1] = jnp.where(odd, lanes(hi, 1), lo)
    send(True, (2, 0, 1), scopy)
    send(inner | at_hi, (3,), scopy)

    @pl.when(at_lo)
    def _():
        pl.semaphore_wait(barrier, expected)
    send(at_lo, (3, 6, 7), copy)
    send(at_lo, (3,), scopy)

    for i in range(2):
        @pl.when(spots[i][1])
        def _():
            arrival(i).wait_recv()
    for n, (f, d) in enumerate(PLANES):
        ref, z0 = fields[f]
        strided(ref, z0, RX + d)[...] = rx[1, n]
        strided(ref, z0, EX - 1 - d)[...] = rx[0, n]
    lane8, lane24 = iota(8, 1), iota(EX, 1)
    group8 = lax.shift_right_logical(lane8, 3)

    def rows(z, packs):
        return tuple(
            jnp.where(group8 == z, lanes(ref[at(z + z0, 8, RX)], 8 * z + 4), pack)
            for (ref, z0), pack in zip(fields, packs))

    tails = lax.fori_loop(0, NZ, rows, (jnp.zeros((8, LY), F32),) * FIELDS, unroll=8)
    whole = [jnp.concatenate([a, b], axis=0) for a, b in zip(packs, tails)]

    def feed(z, v, pack):
        spot = (lane24 - 8 * z) & (LY - 1)
        return jnp.where((spot == 8) | (spot == LY - 1), lanes(v, 8 * z + 4), pack)

    inside = lane24 > 0

    def coefficients(z, carry):
        tz_lo, pack = carry
        k = perm[at(z + 1)]
        tz_hi = harmonic(k, perm[at(z + 2)])
        t_x = harmonic(k, before(k))
        t_y = jnp.where(inside, harmonic(k, lanes(k, 1)), 0.0)
        s = stor[at(z)]
        total = s + t_x + after(t_x) + t_y + lanes(t_y, -1) + tz_lo + tz_hi
        tx[z], ty[z], tz[z] = t_x, t_y, tz_lo
        gain[at(z)] = gain[at(z)] * inverse(jnp.maximum(total, TINY))
        rhs[at(z)] = s * pa[at(z + 1)] + rhs[at(z)]
        return tz_hi, feed(z, k, pack)

    tz[NZ], fed_k = lax.fori_loop(0, NZ, coefficients, (plane, plane), unroll=NZ)

    fed = []
    for it in range(SWEEPS):
        now, new = (pa, pb) if it % 2 == 0 else (pb, pa)

        def sweep(z, carry):
            flow_lo, pack = carry
            p = now[at(z + 1)]
            fx = tx[z] * (p - before(p))
            fy = ty[z] * (p - lanes(p, 1))
            flow_hi = tz[z + 1] * (now[at(z + 2)] - p)
            r = rhs[at(z)] - stor[at(z)] * p - fx + after(fx) - fy + lanes(fy, -1) - flow_lo + flow_hi
            new[at(z + 1)] = p + F32(relax_weight(it)) * gain[at(z)] * r
            return flow_hi, feed(z, p, pack)

        fed.append(lax.fori_loop(0, NZ, sweep, (plane, plane), unroll=NZ)[1])

    for i in range(2, 8):
        @pl.when(spots[i][1])
        def _():
            arrival(i).wait_recv()

    column = lane24 & 7
    low24 = column < 4
    pad2, pad4 = jnp.zeros((2, LY), F32), jnp.zeros((4, LY), F32)
    strips = []
    for d in range(2):
        left, right = rc.at[2 * d], rc.at[2 * d + 1]
        a = jnp.concatenate([ry[d, pl.ds(0, RX)], right[pl.ds(0, 3)], pad2, left[pl.ds(0, 3)]], axis=0)
        b = jnp.concatenate([ry[d, pl.ds(RX, RX)], right[pl.ds(3, 2)], pad4, left[pl.ds(3, 2)]], axis=0)
        m = ry[d, pl.ds(2 * RX, 8)]
        m_tail = [right[pl.ds(5, 2)], pad4, left[pl.ds(5, 2)]]
        if d == 0:
            halos = (a, lanes(a, -4), b, lanes(b, -4), jnp.concatenate([m, lanes(m, -4)] + m_tail, axis=0))
        else:
            halos = (lanes(a, 4), a, lanes(b, 4), b, jnp.concatenate([lanes(m, 4), m] + m_tail, axis=0))
        k, p, s, q, free = (
            jnp.where(low24, h, w) if d == 0 else jnp.where(low24, w, h) for h, w in zip(halos, whole))
        fx_t = harmonic(k, before(k))
        fz_t = jnp.where(lane24 < 8, 0.0, harmonic(k, lanes(k, 8)))
        end = column == (7 if d == 0 else 0)
        turn = -1 if d == 0 else 1
        t_lo = harmonic(k, lanes(k, 1))
        t_end = harmonic(k, lanes(fed_k, turn))
        if d == 0:
            t_hi = jnp.where(end, t_end, lanes(t_lo, -1))
        else:
            t_lo = jnp.where(end, t_end, t_lo)
            t_hi = lanes(t_lo, -1)
        total = s + fx_t + after(fx_t) + t_lo + t_hi + fz_t + lanes(fz_t, -8)
        g = free * inverse(jnp.maximum(total, TINY))
        right_side = s * p + q
        for it in range(SWEEPS):
            p_lo, p_hi = lanes(p, 1), lanes(p, -1)
            beyond = lanes(fed[it], turn)
            if d == 0:
                p_hi = jnp.where(end, beyond, p_hi)
            else:
                p_lo = jnp.where(end, beyond, p_lo)
            fx = fx_t * (p - before(p))
            fz = fz_t * (p - lanes(p, 8))
            r = (right_side - s * p - fx + after(fx) - t_lo * (p - p_lo) + t_hi * (p_hi - p)
                 - fz + lanes(fz, -8))
            p = p + F32(relax_weight(it)) * g * r
        strips.append((t_lo, p))
    face[...] = jnp.where(column == 4, strips[0][0], lanes(strips[1][0], -1))[:RX]
    edge[...] = jnp.where(column == 3, strips[0][1], lanes(strips[1][1], -2))[:RX]
    own_edge = jnp.where(low24, strips[1][1], strips[0][1])
    outer = (lane24 < 3) | (lane24 > LY - 4)

    def overlay(z, c):
        pb[at(z + 1)] = jnp.where(outer, lanes(own_edge, -(8 * z + 4)), pb[at(z + 1)])
        return c

    lax.fori_loop(0, NZ, overlay, 0, unroll=NZ)

    for i in range(4):
        @pl.when(spots[i][1])
        def _():
            sarrival(i).wait_recv()
    m_lo, m_hi = rsy[0], rsy[1]
    side[0] = jnp.where(odd, lanes(m_lo, 1), lanes(m_hi, -1))
    side[1] = jnp.where(odd, m_lo, m_hi)
    row_lo[...] = rsx[0]
    row_hi[...] = rsx[1]
    for i in range(8):
        @pl.when(spots[i][1])
        def _():
            copy(i).wait_send()
            if i < 4:
                scopy(i).wait_send()


def transport_kernel(sp, phi, rea, p_ref, tx, ty, tz, face, edge, side, row_lo, row_hi,
                     conc_out, p_out, phi_out, conc, sem):
    outs = [
        pltpu.make_async_copy(p_ref.at[pl.ds(1, NZ), pl.ds(0, RX)], p_out, sem.at[0]),
        pltpu.make_async_copy(phi, phi_out, sem.at[1]),
    ]
    for c in outs:
        c.start()
    lane, row = iota(RX, 1), iota(RX, 0)
    first, last = lane == 0, lane == LY - 1
    top, bottom = row == 0, row == RX - 1

    def body(z, carry):
        wide = p_ref[z + 1]
        p = wide[:RX]
        turned = lanes(edge[...], -(8 * z + 3))
        t_x = tx[z]
        crossing = lanes(face[...], -(8 * z + 4))
        t_lo = jnp.where(first, crossing, ty[z, :RX])
        t_hi = jnp.where(last, crossing, lanes(t_lo, -1))
        flows = [
            t_x[:RX] * (p - before(wide)[:RX]),
            after(t_x)[:RX] * (p - after(wide)[:RX]),
            t_lo * (p - jnp.where(first, turned, lanes(p, 1))),
            t_hi * (p - jnp.where(last, turned, lanes(p, -1))),
            tz[z, :RX] * (p - p_ref[z, :RX]),
            tz[z + 1, :RX] * (p - p_ref[z + 2, :RX]),
        ]
        scale = TIME_STEP * inverse(phi[z])
        out = jnp.maximum(flows[0], 0.0)
        for f in flows[1:]:
            out = out + jnp.maximum(f, 0.0)
        keep = 1.0 - scale * out
        take = [-scale * jnp.minimum(f, 0.0) for f in flows]
        reaction = rea[z]
        z_lo, z_hi = jnp.maximum(z - 1, 0), jnp.minimum(z + 1, NZ - 1)
        half = side[lax.div(z, 8)]
        for s in range(NSPEC):
            c = sp[s, pl.ds(pl.multiple_of(z * RX, 8), RX)]
            turned_c = lanes(half, -(2 * (lax.rem(z, 8) * 8 + s) + 1))
            total = c * keep
            total = total + take[0] * jnp.where(top, row_lo[s, pl.ds(z, 1)], before(c))
            total = total + take[1] * jnp.where(bottom, row_hi[s, pl.ds(z, 1)], after(c))
            total = total + take[2] * jnp.where(first, turned_c, lanes(c, 1))
            total = total + take[3] * jnp.where(last, turned_c, lanes(c, -1))
            total = total + take[4] * sp[s, pl.ds(pl.multiple_of(z_lo * RX, 8), RX)]
            total = total + take[5] * sp[s, pl.ds(pl.multiple_of(z_hi * RX, 8), RX)]
            if STOICHIOMETRY[s]:
                total = total + STOICHIOMETRY[s] * reaction
            conc[s, z] = total
        return carry

    for part in range(4):
        lax.fori_loop(4 * part, 4 * part + 4, body, 0, unroll=4)
        at = pl.ds(4 * part, 4)
        c = pltpu.make_async_copy(conc.at[:, at], conc_out.at[:, at], sem.at[2 + part])
        c.start()
        outs.append(c)
    for c in outs:
        c.wait()


def build(sizes):
    tile, wide = (NZ, RX, LY), (NZ, EX, LY)
    flat, padded = (NZ * EX, LY), ((NZ + 2) * EX, LY)
    species = (NSPEC, NZ, RX, LY)
    halo = [
        (2, len(PLANES), NZ, LY), (2, 2 * RX + 8, LY), (4, 8, LY), (2, NSPEC, NZ, LY), (2, RX, LY),
    ]
    vmem = pl.BlockSpec(memory_space=pltpu.VMEM)
    hbm = pl.BlockSpec(memory_space=pltpu.HBM)
    middle = [
        (NSPEC, NZ * RX, LY), tile, tile, padded, wide, wide, (NZ + 1, EX, LY),
        (RX, LY), (RX, LY), (2, RX, LY), (NSPEC, NZ, LY), (NSPEC, NZ, LY),
    ]
    dma = pltpu.SemaphoreType.DMA

    def shards(sp, *args):
        args = [pltpu.with_memory_space_constraint(a, pltpu.HBM) for a in (sp.reshape(middle[0]), *args)]
        shared = pl.pallas_call(
            lambda *refs: flow_kernel(sizes, *refs),
            out_shape=[pltpu.VMEM(shape, F32) for shape in middle],
            in_specs=[hbm] * 6,
            out_specs=[vmem] * len(middle),
            scratch_shapes=[
                pltpu.VMEM(tile, F32), pltpu.VMEM(tile, jnp.int32), pltpu.VMEM(tile, jnp.int32),
                pltpu.VMEM(tile, F32), pltpu.VMEM(tile, F32),
                pltpu.VMEM(padded, F32), pltpu.VMEM(padded, F32),
                pltpu.VMEM(flat, F32), pltpu.VMEM(flat, F32), pltpu.VMEM(flat, F32),
                *[pltpu.VMEM(shape, F32) for shape in halo + halo],
                dma((7,)), dma((8,)), dma((8,)), dma((4,)), dma((4,)), pltpu.SemaphoreType.REGULAR,
            ],
            compiler_params=pltpu.CompilerParams(
                collective_id=0, has_side_effects=True, vmem_limit_bytes=32 * 2**20),
            name="flow",
        )(*args)
        shared = list(shared)
        shared[3] = shared[3].reshape(NZ + 2, EX, LY)
        return tuple(pl.pallas_call(
            transport_kernel,
            out_shape=[jax.ShapeDtypeStruct(s, F32) for s in (species, tile, tile)],
            in_specs=[vmem] * len(middle),
            out_specs=[hbm] * 3,
            scratch_shapes=[pltpu.VMEM(species, F32), dma((6,))],
            compiler_params=pltpu.CompilerParams(vmem_limit_bytes=16 * 2**20),
            name="transport",
        )(*shared))

    return shards


def solution(mesh):
    specs = (P(None, None, "gx", "gy"),) + (P(None, "gx", "gy"),) * 5
    outs = (P(None, None, "gx", "gy"), P(None, "gx", "gy"), P(None, "gx", "gy"))
    sizes = (mesh.shape["gx"], mesh.shape["gy"])
    return jax.shard_map(build(sizes), mesh=mesh, in_specs=specs, out_specs=outs, check_vma=False)
```

time: 26.9 us -> 27.5 us (1.022)
  Pallas kernels: 26.1 us -> 26.7 us
    pallas_call x1, Pallas kernels: 1.88 us -> 2.84 us  [shards(): pl.pallas_call(transport_kernel, out_shape=[jax.ShapeDtypeStruct(s, F32)...]
    pallas_call x1, Pallas kernels: 24.2 us -> 23.8 us  [shards(): pl.pallas_call(lambda *refs: flow_kernel(sizes, *refs), out_shape=[pltpu....]
where the time goes in v4:
time: 27.5 us; the launch traced here: 27.3 us
  Pallas kernels  26.7 us (97%)
  between operations  0.64 us (2%)
    pallas_call x1, Pallas kernels, shards(): pl.pallas_call(lambda *refs: flow_kernel(sizes, *refs), out_shape=[pltpu....  23.8 us
    pallas_call x1, Pallas kernels, shards(): pl.pallas_call(transport_kernel, out_shape=[jax.ShapeDtypeStruct(s, F32)...  2.84 us

profile of v4, /device:TPU:30, one launch (start us, length us, event | category | flops | bytes accessed | tf_op | source)
XLA Modules:
  0.0 27.3 jit_solution(12045588718373446280)
XLA Ops:
  0.6 23.8 %flow.1 = (f32[8,256,128]{2,1,0:T(8,128)S(1)}, f32[16,16,128]{2,1,0:T(8,128)S(1)}, f32[16,16,128]{2,1,0:T(8,128)S(1)}, f32[432,128]{1,0:T(8,128)S(1)}, f32[16,24...) custom-call(f32[8,256,128]{2,1,0:T(8,128)} %bitcast.3, ...), custom_call_target="tpu_custom_call" | custom-call | tf_op jit(solution)/shard_map/flow/pallas_call | solution.py:496
  24.5 2.8 %transport.1 = (f32[8,16,16,128]{3,2,1,0:T(8,128)}, f32[16,16,128]{2,1,0:T(8,128)}, f32[16,16,128]{2,1,0:T(8,128)}) custom-call(f32[8,256,128]{2,1,0:T(8,128)S(1)} %get-tuple-element.15.sp, f32[16,16,128]{2,1,0:T(8,128)S(1)} %get-tuple-element.16.phi, f32[16,16,128]{2,1,0:T(8,128)S(1)} %get-tuple-element.17.rea, f32[18,24,128]{2,1,0:T(8,128)S(1)} %bitcast.2, ...), custom_call_target="tpu_custom_call" | custom-call | tf_op jit(solution)/shard_map/transport/pallas_call | solution.py:515

commit v5 on v4

v5 whole, which is shorter than its diff:
```python
import math

import jax
import jax.numpy as jnp
from jax import lax
from jax.experimental import pallas as pl
from jax.experimental.pallas import tpu as pltpu
from jax.sharding import PartitionSpec as P

SWEEPS = 3
NSPEC, NZ, RX, LY = 8, 16, 16, 128
EX = RX + 8
FIELDS = 5
TINY = 1e-30
PLANES = [(f, d) for f in range(FIELDS) for d in range(4 if f < 2 else 3)]

ZONE_RATES = (0.02, 0.05, 0.1, 0.2)
ZONE_PERMEABILITY = (5.0, 10.0, 20.0, 40.0)
SOLUBILITY = 0.5
MOLAR_VOLUME = 0.05
STORAGE_COEF = 0.2
TIME_STEP = 0.2
CHEB_SPREAD = 0.92
STOICHIOMETRY = (-1.0, -1.0, 0.0, 0.0, 0.0, 0.0, 0.0, 0.0)

F32 = jnp.float32
MESH = pl.DeviceIdType.MESH
DIRS = ((-1, 0), (1, 0), (0, -1), (0, 1), (-1, -1), (1, -1), (-1, 1), (1, 1))
OPPOSITE = tuple(DIRS.index((-a, -b)) for a, b in DIRS)


def relax_weight(iteration):
    return 1.0 / (1.0 + CHEB_SPREAD * math.cos(math.pi * (2 * iteration + 1) / (2 * SWEEPS)))


def lookup(labels, table):
    out = jnp.where(labels == 0, F32(table[0]), F32(table[1]))
    out = jnp.where(labels == 2, F32(table[2]), out)
    return jnp.where(labels == 3, F32(table[3]), out)


def inverse(x):
    guess = pl.reciprocal(x, approx=True)
    return guess * (2.0 - x * guess)


def harmonic(a, b):
    return (2.0 * a * b) * inverse(jnp.maximum(a + b, TINY))


def lanes(x, shift):
    return pltpu.roll(x, shift % LY if isinstance(shift, int) else lax.rem(shift + 2 * LY, LY), 1)


def before(x):
    return pltpu.roll(x, 1, 0)


def after(x):
    return pltpu.roll(x, x.shape[0] - 1, 0)


def iota(rows, dim):
    return lax.broadcasted_iota(jnp.int32, (rows, LY), dim)


def flow_kernel(sizes, sp_in, por_in, old_in, src_in, zone_in, fix_in,
                spx, left, right, phi, rea, pd, tx, ty, tz, cross, side,
                sp, por, zone, fix, old, src, pa, p1, p2, perm, stor, rhs, gain, step, known,
                sx, sy, sc, ssx, ssy, rx, ry, rc, rsx, rsy,
                in_sem, send_sem, recv_sem, s_send, s_recv, ready):
    gx, gy = lax.axis_index("gx"), lax.axis_index("gy")
    spots = []
    for dx, dy in DIRS:
        there = None
        for here, move, size in ((gx, dx, sizes[0]), (gy, dy, sizes[1])):
            if move:
                ok = here > 0 if move < 0 else here < size - 1
                there = ok if there is None else there & ok
        spots.append(((gx + dx, gy + dy), there))

    seam = sizes[1] // 2
    split = jnp.bool_(sizes[1] >= 4)
    at_lo, at_hi = (gy == seam - 1) & split, (gy == seam) & split
    at_seam = at_lo | at_hi
    barrier = pltpu.get_barrier_semaphore()
    expected = 0
    for i, (where, there) in enumerate(spots):
        far = (at_lo & (DIRS[i][1] > 0)) | (at_hi & (DIRS[i][1] < 0))
        counts = split & ((where[1] == seam - 1) | (where[1] == seam))
        beside = there & (far | jnp.logical_not(counts))

        @pl.when(beside)
        def _():
            pl.semaphore_signal(barrier, inc=1, device_id=where, device_id_type=MESH)
        expected = expected + (there & (far | jnp.logical_not(at_seam))).astype(jnp.int32)

    loads = [
        pltpu.make_async_copy(sp_in.at[pl.ds(0, 2)], sp.at[pl.ds(0, 2)], in_sem.at[0]),
        pltpu.make_async_copy(zone_in, zone, in_sem.at[1]),
        pltpu.make_async_copy(por_in, por, in_sem.at[2]),
        pltpu.make_async_copy(old_in, old, in_sem.at[3]),
        pltpu.make_async_copy(src_in, src, in_sem.at[4]),
        pltpu.make_async_copy(fix_in, fix, in_sem.at[5]),
        pltpu.make_async_copy(sp_in.at[pl.ds(2, NSPEC - 2)], sp.at[pl.ds(2, NSPEC - 2)], in_sem.at[6]),
    ]
    for c in loads:
        c.start()

    for i in range(8):
        @pl.when(jnp.logical_not(spots[i][1]))
        def _():
            if i < 2:
                rx[i] = jnp.zeros(rx.shape[1:], F32)
                rsx[i] = jnp.zeros(rsx.shape[1:], F32)
            elif i < 4:
                ry[i - 2] = jnp.zeros(ry.shape[1:], F32)
                rsy[i - 2] = jnp.zeros(rsy.shape[1:], F32)
            else:
                rc[i - 4] = jnp.zeros(rc.shape[1:], F32)
    plane = jnp.zeros((EX, LY), F32)
    for ref in (perm, pa, p1, p2, pd):
        ref[pl.ds(0, EX)] = plane
        ref[pl.ds((NZ + 1) * EX, EX)] = plane
    for ref in (stor, rhs, gain):
        for z in range(NZ):
            ref[pl.ds(z * EX + RX, 8)] = plane[:8]

    lane = iota(RX, 1)
    group = lax.shift_right_logical(lane, 3)
    low = (lane & 7) < 4
    for c in loads[:6]:
        c.wait()

    def at(z, rows=EX, skip=0):
        return pl.ds(pl.multiple_of(z * EX + skip, 8), rows)

    def plane_at(r, up=0):
        return pl.ds((1 + up) * EX + r % EX, NZ, stride=EX)

    def feed_mask(z):
        spot = (iota(8, 1) - 8 * z) & (LY - 1)
        return (spot == 8) | (spot == LY - 1)

    def own(z, packs):
        rows = pl.ds(pl.multiple_of(z * RX, 8), RX)
        c0, c1 = sp[0, rows], sp[1, rows]
        label = zone[z]
        reaction = lookup(label, ZONE_RATES) * (c0 * c1 - SOLUBILITY)
        new = por[z] - MOLAR_VOLUME * reaction
        solid = 1.0 - new
        k = lookup(label, ZONE_PERMEABILITY) * (new * new * new) * inverse(solid * solid)
        s = STORAGE_COEF * new
        free = 1.0 - fix[z].astype(F32)
        p, q = old[z], src[z]
        rea[rows] = reaction
        phi[rows] = new
        perm[at(z + 1, RX)] = k
        pa[at(z + 1, RX)] = p
        stor[at(z, RX)] = s
        rhs[at(z, RX)] = q
        gain[at(z, RX)] = free
        turned = [lanes(v, 8 * z + 4) for v in (k, p, s, q, free)]
        mask = feed_mask(z)
        fed_new = [jnp.where(mask, turned[f][8 * t:8 * t + 8], packs[FIELDS + 2 * f + t]) for f in range(2) for t in range(2)]
        return tuple(jnp.where(group == z, v, pack) for v, pack in zip(turned, packs)) + tuple(fed_new)

    zero, zero8 = jnp.zeros((RX, LY), F32), jnp.zeros((8, LY), F32)
    packs = lax.fori_loop(0, NZ, own, (zero,) * FIELDS + (zero8,) * 4, unroll=8)
    own_fed = packs[FIELDS:]
    packs = packs[:FIELDS]
    k, p, s, q, free = packs
    low8 = low[:8]
    for side_y in range(2):
        if side_y == 0:
            a, b = jnp.where(low, lanes(k, -4), p), jnp.where(low, lanes(s, -4), q)
            m = jnp.where(low8, lanes(free[:8], -4), free[8:])
        else:
            a, b = jnp.where(low, k, lanes(p, 4)), jnp.where(low, s, lanes(q, 4))
            m = jnp.where(low8, free[:8], lanes(free[8:], 4))
        sy[side_y, pl.ds(0, RX)] = a
        sy[side_y, pl.ds(RX, RX)] = b
        sy[side_y, pl.ds(2 * RX, 8)] = m
        for side_x in range(2):
            j = 2 * side_y + side_x
            if side_x == 0:
                parts_c = (a[:3], b[:2], free[:2])
            else:
                parts_c = (a[RX - 3:], b[RX - 2:], free[RX - 2:])
            sc[j, pl.ds(0, 3)] = parts_c[0]
            sc[j, pl.ds(3, 2)] = parts_c[1]
            sc[j, pl.ds(5, 2)] = parts_c[2]
            sc[j, pl.ds(7, 1)] = parts_c[2][:1]

    def strided(ref, z0, row):
        return ref.at[pl.ds(z0 * EX + row, NZ, stride=EX)]

    fields = ((perm, 1), (pa, 1), (stor, 0), (rhs, 0), (gain, 0))
    for n, (f, d) in enumerate(PLANES):
        ref, z0 = fields[f]
        sx[0, n] = strided(ref, z0, d)[...]
        sx[1, n] = strided(ref, z0, RX - 1 - d)[...]

    def parts(i):
        if i < 2:
            return sx.at[i], rx, i
        if i < 4:
            return sy.at[i - 2], ry, i - 2
        return sc.at[i - 4], rc, i - 4

    def copy(i):
        from_ref, _, _ = parts(i)
        _, dst, slot = parts(OPPOSITE[i])
        return pltpu.make_async_remote_copy(
            src_ref=from_ref, dst_ref=dst.at[slot], send_sem=send_sem.at[i],
            recv_sem=recv_sem.at[OPPOSITE[i]], device_id=spots[i][0], device_id_type=MESH)

    def arrival(i):
        from_ref, dst, slot = parts(i)
        return pltpu.make_async_remote_copy(
            src_ref=from_ref, dst_ref=dst.at[slot], send_sem=send_sem.at[i],
            recv_sem=recv_sem.at[i], device_id=spots[i][0], device_id_type=MESH)

    def sparts(i):
        return (ssx.at[i], rsx, i) if i < 2 else (ssy.at[i - 2], rsy, i - 2)

    def scopy(i):
        from_ref, _, _ = sparts(i)
        _, dst, slot = sparts(OPPOSITE[i])
        return pltpu.make_async_remote_copy(
            src_ref=from_ref, dst_ref=dst.at[slot], send_sem=s_send.at[i],
            recv_sem=s_recv.at[OPPOSITE[i]], device_id=spots[i][0], device_id_type=MESH)

    def sarrival(i):
        from_ref, dst, slot = sparts(i)
        return pltpu.make_async_remote_copy(
            src_ref=from_ref, dst_ref=dst.at[slot], send_sem=s_send.at[i],
            recv_sem=s_recv.at[i], device_id=spots[i][0], device_id_type=MESH)

    def send(only, order, make):
        for i in order:
            @pl.when(spots[i][1] & only)
            def _():
                make(i).start()

    inner = jnp.logical_not(at_seam)

    @pl.when(at_hi)
    def _():
        pl.semaphore_wait(barrier, expected)
    send(at_hi, (2, 4, 5), copy)

    loads[6].wait()
    for s in range(NSPEC):
        ssx[0, s] = sp[s, pl.ds(0, NZ, stride=RX)]
        ssx[1, s] = sp[s, pl.ds(RX - 1, NZ, stride=RX)]
    pair = lax.shift_right_logical(lane, 1)
    odd = (lane & 1) == 1

    halves = [zero, zero]
    for x in range(RX):
        for s in range(NSPEC):
            m = (x % 8) * 8 + s
            turned = lanes(sp[s, pl.ds(x, NZ, stride=RX)], 2 * m + 1)
            halves[x // 8] = jnp.where(pair == m, turned, halves[x // 8])
    lo, hi = halves
    ssy[0] = jnp.where(odd, lo, lanes(hi, -1))
    ssy[1] = jnp.where(odd, lanes(hi, 1), lo)
    send(at_hi, (2,), scopy)

    @pl.when(inner)
    def _():
        pl.semaphore_wait(barrier, expected)
    for edge_row, toward in ((seam - 2, 1), (seam + 1, -1)):
        @pl.when((gy == edge_row) & split)
        def _():
            pl.semaphore_signal(ready, inc=1, device_id=(gx, gy + toward), device_id_type=MESH)

    @pl.when(at_seam)
    def _():
        pl.semaphore_wait(ready, 1)
    send(True, (0, 1), copy)
    send(inner | at_lo, (2, 4, 5), copy)
    send(inner | at_hi, (3, 6, 7), copy)

    send(True, (0, 1), scopy)
    send(inner | at_lo, (2,), scopy)
    send(inner | at_hi, (3,), scopy)

    for s in range(NSPEC):
        for x in range(RX):
            c = sp[s, pl.ds(x, NZ, stride=RX)]
            spx[s, pl.ds(NZ * (x + 1), NZ)] = c
            left[s, pl.ds(NZ * x, NZ)] = lanes(c, 1)
            right[s, pl.ds(NZ * x, NZ)] = lanes(c, -1)

    def face_x(r):
        tx[r % EX] = harmonic(perm[plane_at(r)], perm[plane_at(r - 1)])

    def in_plane(r):
        k = perm[plane_at(r)]
        ty[0, r % EX] = jnp.where(lane > 0, harmonic(k, lanes(k, 1)), 0.0)
        ty[1, r % EX] = jnp.where(lane < LY - 1, harmonic(k, lanes(k, -1)), 0.0)
        tz[0, r % EX] = harmonic(k, perm[plane_at(r, -1)])
        tz[1, r % EX] = harmonic(k, perm[plane_at(r, 1)])

    def coefficients(r):
        at_r = r % EX
        s = stor[plane_at(r, -1)]
        total = (s + tx[at_r] + tx[(r + 1) % EX]) + (ty[0, at_r] + ty[1, at_r]) + (tz[0, at_r] + tz[1, at_r])
        step[at_r] = gain[plane_at(r, -1)] * inverse(jnp.maximum(total, TINY))
        known[at_r] = s * pa[plane_at(r)] + rhs[plane_at(r, -1)]

    def relax(it, r):
        now, new, at_r = levels[it], levels[it + 1], r % EX
        p = now[plane_at(r)]
        out = stor[plane_at(r, -1)] * p
        out = out + tx[at_r] * (p - now[plane_at(r - 1)])
        out = out + tx[(r + 1) % EX] * (p - now[plane_at(r + 1)])
        out = out + tz[0, at_r] * (p - now[plane_at(r, -1)])
        out = out + tz[1, at_r] * (p - now[plane_at(r, 1)])
        out = out + ty[0, at_r] * (p - lanes(p, 1))
        out = out + ty[1, at_r] * (p - lanes(p, -1))
        new[plane_at(r)] = p + F32(relax_weight(it)) * step[at_r] * (known[at_r] - out)

    levels = (pa, p1, p2, pd)
    for r in range(1, RX):
        face_x(r)
    for r in range(RX):
        in_plane(r)
    for r in range(1, RX - 1):
        coefficients(r)
    for it in range(SWEEPS):
        for r in range(1 + it, RX - 1 - it):
            relax(it, r)

    @pl.when(at_lo)
    def _():
        pl.semaphore_wait(barrier, expected)
    send(at_lo, (3, 6, 7), copy)
    send(at_lo, (3,), scopy)

    for i in range(2):
        @pl.when(spots[i][1])
        def _():
            arrival(i).wait_recv()
    for n, (f, d) in enumerate(PLANES):
        ref, z0 = fields[f]
        strided(ref, z0, RX + d)[...] = rx[1, n]
        strided(ref, z0, EX - 1 - d)[...] = rx[0, n]
    for r in (-3, -2, -1, 0, RX, RX + 1, RX + 2, RX + 3):
        face_x(r)
    for r in (-3, -2, -1, RX, RX + 1, RX + 2):
        in_plane(r)
    for r in (-3, -2, -1, 0, RX - 1, RX, RX + 1, RX + 2):
        coefficients(r)
    for it in range(SWEEPS):
        for j in range(4):
            relax(it, it - 3 + j)
            relax(it, RX - 1 - it + j)

    lane24 = iota(EX, 1)
    group8 = lax.shift_right_logical(iota(8, 1), 3)
    tails, tail_fed, fed_1, fed_2 = [zero8] * FIELDS, [zero8] * 2, [zero8] * 3, [zero8] * 3
    for z in range(NZ):
        mask = feed_mask(z)
        for f, (ref, z0) in enumerate(fields):
            turned = lanes(ref[at(z + z0, 8, RX)], 8 * z + 4)
            tails[f] = jnp.where(group8 == z, turned, tails[f])
            if f < 2:
                tail_fed[f] = jnp.where(mask, turned, tail_fed[f])
        for ref, pack in ((p1, fed_1), (p2, fed_2)):
            for t in range(3):
                pack[t] = jnp.where(mask, lanes(ref[at(z + 1, 8, 8 * t)], 8 * z + 4), pack[t])
    whole = [jnp.concatenate([a, b], axis=0) for a, b in zip(packs, tails)]
    fed_k = jnp.concatenate([own_fed[0], own_fed[1], tail_fed[0]], axis=0)
    fed = [
        jnp.concatenate([own_fed[2], own_fed[3], tail_fed[1]], axis=0),
        jnp.concatenate(fed_1, axis=0), jnp.concatenate(fed_2, axis=0),
    ]

    for i in range(2, 8):
        @pl.when(spots[i][1])
        def _():
            arrival(i).wait_recv()

    column = lane24 & 7
    low24 = column < 4
    pad2, pad4 = jnp.zeros((2, LY), F32), jnp.zeros((4, LY), F32)
    strips = []
    for d in range(2):
        minus, plus = rc.at[2 * d], rc.at[2 * d + 1]
        a = jnp.concatenate([ry[d, pl.ds(0, RX)], plus[pl.ds(0, 3)], pad2, minus[pl.ds(0, 3)]], axis=0)
        b = jnp.concatenate([ry[d, pl.ds(RX, RX)], plus[pl.ds(3, 2)], pad4, minus[pl.ds(3, 2)]], axis=0)
        m = ry[d, pl.ds(2 * RX, 8)]
        m_tail = [plus[pl.ds(5, 2)], pad4, minus[pl.ds(5, 2)]]
        if d == 0:
            halos = (a, lanes(a, -4), b, lanes(b, -4), jnp.concatenate([m, lanes(m, -4)] + m_tail, axis=0))
        else:
            halos = (lanes(a, 4), a, lanes(b, 4), b, jnp.concatenate([lanes(m, 4), m] + m_tail, axis=0))
        k, p, s, q, free = (
            jnp.where(low24, h, w) if d == 0 else jnp.where(low24, w, h) for h, w in zip(halos, whole))
        end = column == (7 if d == 0 else 0)
        turn = -1 if d == 0 else 1
        beyond = [lanes(v, turn) for v in [fed_k] + fed]

        def sides(v, outer_v):
            lo, hi = lanes(v, 1), lanes(v, -1)
            if d == 0:
                hi = jnp.where(end, outer_v, hi)
            else:
                lo = jnp.where(end, outer_v, lo)
            return before(v), after(v), lo, hi, lanes(v, 8), lanes(v, -8)

        terms = [harmonic(k, v) for v in sides(k, beyond[0])]
        terms[4] = jnp.where(lane24 < 8, 0.0, terms[4])
        terms[5] = jnp.where(lane24 < LY - 8, terms[5], 0.0)
        total = s + ((terms[0] + terms[1]) + (terms[2] + terms[3])) + (terms[4] + terms[5])
        g = free * inverse(jnp.maximum(total, TINY))
        right_side = s * p + q
        for it in range(SWEEPS):
            flows = [t * (p - v) for t, v in zip(terms, sides(p, beyond[1 + it]))]
            r = (right_side - s * p) - ((flows[0] + flows[1]) + (flows[2] + flows[3])) - (flows[4] + flows[5])
            p = p + F32(relax_weight(it)) * g * r
        across = terms[2] * (p - lanes(p, 1)) if d == 0 else terms[3] * (p - lanes(p, -1))
        strips.append((across, p))
    own_edge = jnp.where(low24, strips[1][1], strips[0][1])
    own_flow = jnp.where(low24, strips[1][0], strips[0][0])
    outer = (lane24 < 3) | (lane24 > LY - 4)
    for z in range(NZ):
        pd[at(z + 1)] = jnp.where(outer, lanes(own_edge, -(8 * z + 4)), pd[at(z + 1)])
        cross[at(z, RX)] = lanes(own_flow[:RX], -(8 * z + 4))

    for i in range(4):
        @pl.when(spots[i][1])
        def _():
            sarrival(i).wait_recv()
    m_lo, m_hi = rsy[0], rsy[1]
    side[0] = jnp.where(odd, lanes(m_lo, 1), lanes(m_hi, -1))
    side[1] = jnp.where(odd, m_lo, m_hi)
    for s in range(NSPEC):
        spx[s, pl.ds(0, NZ)] = rsx[0, s]
        spx[s, pl.ds(NZ * (RX + 1), NZ)] = rsx[1, s]
    for i in range(8):
        @pl.when(spots[i][1])
        def _():
            copy(i).wait_send()
            if i < 4:
                scopy(i).wait_send()


def transport_kernel(spx, left, right, phi, rea, p_ref, tx, ty, tz, cross, side,
                     conc_out, p_out, phi_out, conc, final, weight, sem):
    outs = [pltpu.make_async_copy(phi, phi_out, sem.at[0]), pltpu.make_async_copy(final, p_out, sem.at[1])]
    outs[0].start()
    lane = iota(RX, 1)
    first, last = lane == 0, lane == LY - 1

    def plane_at(r, up=0):
        return pl.ds((1 + up) * EX + r % EX, NZ, stride=EX)

    for x in range(RX):
        p = p_ref[plane_at(x)]
        final[pl.ds(x, NZ, stride=RX)] = p
        through = cross[plane_at(x, -1)]
        flows = [
            tx[x] * (p - p_ref[plane_at(x - 1)]),
            tx[x + 1] * (p - p_ref[plane_at(x + 1)]),
            jnp.where(first, through, ty[0, x] * (p - lanes(p, 1))),
            jnp.where(last, through, ty[1, x] * (p - lanes(p, -1))),
            tz[0, x] * (p - p_ref[plane_at(x, -1)]),
            tz[1, x] * (p - p_ref[plane_at(x, 1)]),
        ]
        scale = TIME_STEP * inverse(phi[pl.ds(x, NZ, stride=RX)])
        out = [jnp.maximum(f, 0.0) for f in flows]
        out = ((out[0] + out[1]) + (out[2] + out[3])) + (out[4] + out[5])
        weight[0, x] = 1.0 - scale * out
        for n, f in enumerate(flows):
            weight[n + 1, x] = -scale * jnp.minimum(f, 0.0)
    outs[1].start()

    group = 2
    for s0 in range(0, NSPEC, group):
        for x in range(RX):
            w = [weight[n, x] for n in range(7)]
            for s in range(s0, s0 + group):
                def row(shift):
                    return spx[s, pl.ds(NZ * (x + 1) + shift, NZ)]

                turned = lanes(side[x // 8], -(2 * ((x % 8) * 8 + s) + 1))
                around = [
                    row(-NZ), row(NZ),
                    jnp.where(first, turned, left[s, pl.ds(NZ * x, NZ)]),
                    jnp.where(last, turned, right[s, pl.ds(NZ * x, NZ)]),
                    row(-1), row(1),
                ]
                total = row(0) * w[0]
                for a, b in zip(w[1:], around):
                    total = total + a * b
                if STOICHIOMETRY[s]:
                    total = total + STOICHIOMETRY[s] * rea[pl.ds(x, NZ, stride=RX)]
                conc[s, pl.ds(x, NZ, stride=RX)] = total
        some = pl.ds(s0, group)
        c = pltpu.make_async_copy(conc.at[some], conc_out.at[some], sem.at[2 + s0 // group])
        c.start()
        outs.append(c)
    for c in outs:
        c.wait()


def build(sizes):
    tile, rows = (NZ, RX, LY), (NZ * RX, LY)
    flat, padded, planes = (NZ * EX, LY), ((NZ + 2) * EX, LY), (EX, NZ, LY)
    species, turned = (NSPEC, NZ, RX, LY), (NSPEC, NZ * RX, LY)
    halo = [
        (2, len(PLANES), NZ, LY), (2, 2 * RX + 8, LY), (4, 8, LY), (2, NSPEC, NZ, LY), (2, NZ, LY),
    ]
    vmem = pl.BlockSpec(memory_space=pltpu.VMEM)
    hbm = pl.BlockSpec(memory_space=pltpu.HBM)
    middle = [
        (NSPEC, (RX + 2) * NZ, LY), turned, turned, rows, rows, padded, planes, (2,) + planes, (2,) + planes,
        flat, (2, NZ, LY),
    ]
    dma = pltpu.SemaphoreType.DMA

    def shards(sp, *args):
        args = [pltpu.with_memory_space_constraint(a, pltpu.HBM) for a in (sp.reshape(turned), *args)]
        shared = pl.pallas_call(
            lambda *refs: flow_kernel(sizes, *refs),
            out_shape=[pltpu.VMEM(shape, F32) for shape in middle],
            in_specs=[hbm] * 6,
            out_specs=[vmem] * len(middle),
            scratch_shapes=[
                pltpu.VMEM(turned, F32),
                pltpu.VMEM(tile, F32), pltpu.VMEM(tile, jnp.int32), pltpu.VMEM(tile, jnp.int32),
                pltpu.VMEM(tile, F32), pltpu.VMEM(tile, F32),
                *[pltpu.VMEM(padded, F32)] * 4, *[pltpu.VMEM(flat, F32)] * 3, *[pltpu.VMEM(planes, F32)] * 2,
                *[pltpu.VMEM(shape, F32) for shape in halo + halo],
                dma((7,)), dma((8,)), dma((8,)), dma((4,)), dma((4,)), pltpu.SemaphoreType.REGULAR,
            ],
            compiler_params=pltpu.CompilerParams(
                collective_id=0, has_side_effects=True, vmem_limit_bytes=32 * 2**20),
            name="flow",
        )(*args)
        conc, pressure, porosity = pl.pallas_call(
            transport_kernel,
            out_shape=[jax.ShapeDtypeStruct(s, F32) for s in (turned, rows, rows)],
            in_specs=[vmem] * len(middle),
            out_specs=[hbm] * 3,
            scratch_shapes=[pltpu.VMEM(turned, F32), pltpu.VMEM(rows, F32), pltpu.VMEM((7, RX, NZ, LY), F32), dma((6,))],
            compiler_params=pltpu.CompilerParams(vmem_limit_bytes=16 * 2**20),
            name="transport",
        )(*shared)
        return conc.reshape(species), pressure.reshape(tile), porosity.reshape(tile)

    return shards


def solution(mesh):
    specs = (P(None, None, "gx", "gy"),) + (P(None, "gx", "gy"),) * 5
    outs = (P(None, None, "gx", "gy"), P(None, "gx", "gy"), P(None, "gx", "gy"))
    sizes = (mesh.shape["gx"], mesh.shape["gy"])
    return jax.shard_map(build(sizes), mesh=mesh, in_specs=specs, out_specs=outs, check_vma=False)
```

time: 27.5 us -> 22.6 us (0.82)
  the two profiles are of different devices: /device:TPU:30 before, /device:TPU:6 now
where the time goes in v5:
time: 22.6 us; the launch traced here: 22.5 us
  Pallas kernels  21.8 us (96%)
  between operations  0.64 us (3%)
    pallas_call x1, Pallas kernels, shards(): pl.pallas_call(lambda *refs: flow_kernel(sizes, *refs), out_shape=[pltpu....  20 us
    pallas_call x1, Pallas kernels, shards(): pl.pallas_call(transport_kernel, out_shape=[jax.ShapeDtypeStruct(s, F32)...  1.8 us

profile of v5, /device:TPU:6, one launch (start us, length us, event | category | flops | bytes accessed | tf_op | source)
XLA Modules:
  0.0 22.5 jit_solution(15344334562927249716)
XLA Ops:
  0.6 20.0 %flow.1 = (f32[8,288,128]{2,1,0:T(8,128)S(1)}, f32[8,256,128]{2,1,0:T(8,128)S(1)}, f32[8,256,128]{2,1,0:T(8,128)S(1)}, f32[256,128]{1,0:T(8,128)S(1)}, f32[256,1...) custom-call(f32[8,256,128]{2,1,0:T(8,128)} %bitcast.4, ...), custom_call_target="tpu_custom_call" | custom-call | tf_op jit(solution)/shard_map/flow/pallas_call | solution.py:528
  20.7 1.8 %transport.1 = (f32[8,256,128]{2,1,0:T(8,128)}, f32[256,128]{1,0:T(8,128)}, f32[256,128]{1,0:T(8,128)}) custom-call(f32[8,288,128]{2,1,0:T(8,128)S(1)} %get-tuple-element.17.spx, f32[8,256,128]{2,1,0:T(8,128)S(1)} %get-tuple-element.18.left, f32[8,256,128]{2,1,0:T(8,128)S(1)} %get-tuple-element.19.right, f32[256,128]{1,0:T(8,128)S(1)} %get-tuple-element.20.phi, ...), custom_call_target="tpu_custom_call" | custom-call | tf_op jit(solution)/shard_map/transport/pallas_call | solution.py:545

commit v6 on v5

--- a/solution.py
+++ b/solution.py
@@ -12,6 +12,7 @@
 EX = RX + 8
 FIELDS = 5
 TINY = 1e-30
+CUTS = (1, 1)
 PLANES = [(f, d) for f in range(FIELDS) for d in range(4 if f < 2 else 3)]
 
 ZONE_RATES = (0.02, 0.05, 0.1, 0.2)
@@ -65,8 +66,8 @@
 
 
 def flow_kernel(sizes, sp_in, por_in, old_in, src_in, zone_in, fix_in,
-                spx, left, right, phi, rea, pd, tx, ty, tz, cross, side,
-                sp, por, zone, fix, old, src, pa, p1, p2, perm, stor, rhs, gain, step, known,
+                spx, left, right, phi, rea, final, weight, side,
+                pd, tx, ty, tz, cross, sp, por, zone, fix, old, src, pa, p1, p2, perm, stor, rhs, gain, step, known,
                 sx, sy, sc, ssx, ssy, rx, ry, rc, rsx, rsy,
                 in_sem, send_sem, recv_sem, s_send, s_recv, ready):
     gx, gy = lax.axis_index("gx"), lax.axis_index("gy")
@@ -208,12 +209,22 @@
             return sy.at[i - 2], ry, i - 2
         return sc.at[i - 4], rc, i - 4
 
+    def pieces(i, from_ref, dst, slot, spans, sems):
+        return [
+            pltpu.make_async_remote_copy(
+                src_ref=from_ref.at[span], dst_ref=dst.at[slot, span], send_sem=sems[0].at[i],
+                recv_sem=sems[1].at[OPPOSITE[i]], device_id=spots[i][0], device_id_type=MESH)
+            for span in spans]
+
+    def spans(length, parts_of):
+        cuts = [length * n // parts_of for n in range(parts_of + 1)]
+        return [pl.ds(a, b - a) for a, b in zip(cuts[:-1], cuts[1:])]
+
     def copy(i):
         from_ref, _, _ = parts(i)
         _, dst, slot = parts(OPPOSITE[i])
-        return pltpu.make_async_remote_copy(
-            src_ref=from_ref, dst_ref=dst.at[slot], send_sem=send_sem.at[i],
-            recv_sem=recv_sem.at[OPPOSITE[i]], device_id=spots[i][0], device_id_type=MESH)
+        cut = spans(len(PLANES), CUTS[0]) if i < 2 else spans(from_ref.shape[0], 1)
+        return pieces(i, from_ref, dst, slot, cut, (send_sem, recv_sem))
 
     def arrival(i):
         from_ref, dst, slot = parts(i)
@@ -227,9 +238,8 @@
     def scopy(i):
         from_ref, _, _ = sparts(i)
         _, dst, slot = sparts(OPPOSITE[i])
-        return pltpu.make_async_remote_copy(
-            src_ref=from_ref, dst_ref=dst.at[slot], send_sem=s_send.at[i],
-            recv_sem=s_recv.at[OPPOSITE[i]], device_id=spots[i][0], device_id_type=MESH)
+        cut = spans(NSPEC, CUTS[1]) if i < 2 else spans(NZ, 1)
+        return pieces(i, from_ref, dst, slot, cut, (s_send, s_recv))
 
     def sarrival(i):
         from_ref, dst, slot = sparts(i)
@@ -241,7 +251,8 @@
         for i in order:
             @pl.when(spots[i][1] & only)
             def _():
-                make(i).start()
+                for c in make(i):
+                    c.start()
 
     inner = jnp.logical_not(at_seam)
 
@@ -279,11 +290,15 @@
     @pl.when(at_seam)
     def _():
         pl.semaphore_wait(ready, 1)
-    send(True, (0, 1), copy)
+    later = lax.rem(gx, 16) == 14
+    soon = jnp.logical_not(later)
+    send(True, (1,), copy)
+    send(soon, (0,), copy)
     send(inner | at_lo, (2, 4, 5), copy)
     send(inner | at_hi, (3, 6, 7), copy)
 
-    send(True, (0, 1), scopy)
+    send(True, (1,), scopy)
+    send(soon, (0,), scopy)
     send(inner | at_lo, (2,), scopy)
     send(inner | at_hi, (3,), scopy)
 
@@ -333,6 +348,9 @@
     for it in range(SWEEPS):
         for r in range(1 + it, RX - 1 - it):
             relax(it, r)
+
+    send(later, (0,), copy)
+    send(later, (0,), scopy)
 
     @pl.when(at_lo)
     def _():
@@ -431,6 +449,26 @@
         pd[at(z + 1)] = jnp.where(outer, lanes(own_edge, -(8 * z + 4)), pd[at(z + 1)])
         cross[at(z, RX)] = lanes(own_flow[:RX], -(8 * z + 4))
 
+    first, last = lane == 0, lane == LY - 1
+    for x in range(RX):
+        p = pd[plane_at(x)]
+        final[pl.ds(x, NZ, stride=RX)] = p
+        through = cross[plane_at(x, -1)]
+        flows = [
+            tx[x] * (p - pd[plane_at(x - 1)]),
+            tx[x + 1] * (p - pd[plane_at(x + 1)]),
+            jnp.where(first, through, ty[0, x] * (p - lanes(p, 1))),
+            jnp.where(last, through, ty[1, x] * (p - lanes(p, -1))),
+            tz[0, x] * (p - pd[plane_at(x, -1)]),
+            tz[1, x] * (p - pd[plane_at(x, 1)]),
+        ]
+        scale = TIME_STEP * inverse(phi[pl.ds(x, NZ, stride=RX)])
+        out = [jnp.maximum(f, 0.0) for f in flows]
+        out = ((out[0] + out[1]) + (out[2] + out[3])) + (out[4] + out[5])
+        weight[0, x] = 1.0 - scale * out
+        for n, f in enumerate(flows):
+            weight[n + 1, x] = -scale * jnp.minimum(f, 0.0)
+
     for i in range(4):
         @pl.when(spots[i][1])
         def _():
@@ -444,41 +482,17 @@
     for i in range(8):
         @pl.when(spots[i][1])
         def _():
-            copy(i).wait_send()
+            arrival(i).wait_send()
             if i < 4:
-                scopy(i).wait_send()
-
-
-def transport_kernel(spx, left, right, phi, rea, p_ref, tx, ty, tz, cross, side,
-                     conc_out, p_out, phi_out, conc, final, weight, sem):
+                sarrival(i).wait_send()
+
+
+def transport_kernel(spx, left, right, phi, rea, final, weight, side, conc_out, p_out, phi_out, conc, sem):
     outs = [pltpu.make_async_copy(phi, phi_out, sem.at[0]), pltpu.make_async_copy(final, p_out, sem.at[1])]
-    outs[0].start()
+    for c in outs:
+        c.start()
     lane = iota(RX, 1)
     first, last = lane == 0, lane == LY - 1
-
-    def plane_at(r, up=0):
-        return pl.ds((1 + up) * EX + r % EX, NZ, stride=EX)
-
-    for x in range(RX):
-        p = p_ref[plane_at(x)]
-        final[pl.ds(x, NZ, stride=RX)] = p
-        through = cross[plane_at(x, -1)]
-        flows = [
-            tx[x] * (p - p_ref[plane_at(x - 1)]),
-            tx[x + 1] * (p - p_ref[plane_at(x + 1)]),
-            jnp.where(first, through, ty[0, x] * (p - lanes(p, 1))),
-            jnp.where(last, through, ty[1, x] * (p - lanes(p, -1))),
-            tz[0, x] * (p - p_ref[plane_at(x, -1)]),
-            tz[1, x] * (p - p_ref[plane_at(x, 1)]),
-        ]
-        scale = TIME_STEP * inverse(phi[pl.ds(x, NZ, stride=RX)])
-        out = [jnp.maximum(f, 0.0) for f in flows]
-        out = ((out[0] + out[1]) + (out[2] + out[3])) + (out[4] + out[5])
-        weight[0, x] = 1.0 - scale * out
-        for n, f in enumerate(flows):
-            weight[n + 1, x] = -scale * jnp.minimum(f, 0.0)
-    outs[1].start()
-
     group = 2
     for s0 in range(0, NSPEC, group):
         for x in range(RX):
@@ -518,8 +532,7 @@
     vmem = pl.BlockSpec(memory_space=pltpu.VMEM)
     hbm = pl.BlockSpec(memory_space=pltpu.HBM)
     middle = [
-        (NSPEC, (RX + 2) * NZ, LY), turned, turned, rows, rows, padded, planes, (2,) + planes, (2,) + planes,
-        flat, (2, NZ, LY),
+        (NSPEC, (RX + 2) * NZ, LY), turned, turned, rows, rows, rows, (7, RX, NZ, LY), (2, NZ, LY),
     ]
     dma = pltpu.SemaphoreType.DMA
 
@@ -531,7 +544,8 @@
             in_specs=[hbm] * 6,
             out_specs=[vmem] * len(middle),
             scratch_shapes=[
-                pltpu.VMEM(turned, F32),
+                pltpu.VMEM(padded, F32), pltpu.VMEM(planes, F32), pltpu.VMEM((2,) + planes, F32),
+                pltpu.VMEM((2,) + planes, F32), pltpu.VMEM(flat, F32), pltpu.VMEM(turned, F32),
                 pltpu.VMEM(tile, F32), pltpu.VMEM(tile, jnp.int32), pltpu.VMEM(tile, jnp.int32),
                 pltpu.VMEM(tile, F32), pltpu.VMEM(tile, F32),
                 *[pltpu.VMEM(padded, F32)] * 4, *[pltpu.VMEM(flat, F32)] * 3, *[pltpu.VMEM(planes, F32)] * 2,
@@ -547,7 +561,7 @@
             out_shape=[jax.ShapeDtypeStruct(s, F32) for s in (turned, rows, rows)],
             in_specs=[vmem] * len(middle),
             out_specs=[hbm] * 3,
-            scratch_shapes=[pltpu.VMEM(turned, F32), pltpu.VMEM(rows, F32), pltpu.VMEM((7, RX, NZ, LY), F32), dma((6,))],
+            scratch_shapes=[pltpu.VMEM(turned, F32), dma((6,))],
             compiler_params=pltpu.CompilerParams(vmem_limit_bytes=16 * 2**20),
             name="transport",
         )(*shared)

time: 22.6 us -> 22.2 us (0.982)
  the two profiles are of different devices: /device:TPU:6 before, /device:TPU:289 now
where the time goes in v6:
time: 22.2 us; the launch traced here: 22.1 us
  Pallas kernels  21.5 us (97%)
  between operations  0.64 us (3%)
    pallas_call x1, Pallas kernels, shards(): pl.pallas_call(lambda *refs: flow_kernel(sizes, *refs), out_shape=[pltpu....  20 us
    pallas_call x1, Pallas kernels, shards(): pl.pallas_call(transport_kernel, out_shape=[jax.ShapeDtypeStruct(s, F32)...  1.45 us

profile of v6, /device:TPU:289, one launch (start us, length us, event | category | flops | bytes accessed | tf_op | source)
XLA Modules:
  0.0 22.1 jit_solution(11778149560899352716)
XLA Ops:
  0.6 20.0 %flow.1 = (f32[8,288,128]{2,1,0:T(8,128)S(1)}, f32[8,256,128]{2,1,0:T(8,128)S(1)}, f32[8,256,128]{2,1,0:T(8,128)S(1)}, f32[256,128]{1,0:T(8,128)S(1)}, f32[256,1...) custom-call(f32[8,256,128]{2,1,0:T(8,128)} %bitcast.4, ...), custom_call_target="tpu_custom_call" | custom-call | tf_op jit(solution)/shard_map/flow/pallas_call | solution.py:541
  20.6 1.5 %transport.1 = (f32[8,256,128]{2,1,0:T(8,128)}, f32[256,128]{1,0:T(8,128)}, f32[256,128]{1,0:T(8,128)}) custom-call(f32[8,288,128]{2,1,0:T(8,128)S(1)} %get-tuple-element.14.spx, f32[8,256,128]{2,1,0:T(8,128)S(1)} %get-tuple-element.15.left, f32[8,256,128]{2,1,0:T(8,128)S(1)} %get-tuple-element.16.right, f32[256,128]{1,0:T(8,128)S(1)} %get-tuple-element.17.phi, ...), custom_call_target="tpu_custom_call" | custom-call | tf_op jit(solution)/shard_map/transport/pallas_call | solution.py:559

commit v7 on v6

--- a/solution.py
+++ b/solution.py
@@ -80,22 +80,6 @@
                 there = ok if there is None else there & ok
         spots.append(((gx + dx, gy + dy), there))
 
-    seam = sizes[1] // 2
-    split = jnp.bool_(sizes[1] >= 4)
-    at_lo, at_hi = (gy == seam - 1) & split, (gy == seam) & split
-    at_seam = at_lo | at_hi
-    barrier = pltpu.get_barrier_semaphore()
-    expected = 0
-    for i, (where, there) in enumerate(spots):
-        far = (at_lo & (DIRS[i][1] > 0)) | (at_hi & (DIRS[i][1] < 0))
-        counts = split & ((where[1] == seam - 1) | (where[1] == seam))
-        beside = there & (far | jnp.logical_not(counts))
-
-        @pl.when(beside)
-        def _():
-            pl.semaphore_signal(barrier, inc=1, device_id=where, device_id_type=MESH)
-        expected = expected + (there & (far | jnp.logical_not(at_seam))).astype(jnp.int32)
-
     loads = [
         pltpu.make_async_copy(sp_in.at[pl.ds(0, 2)], sp.at[pl.ds(0, 2)], in_sem.at[0]),
         pltpu.make_async_copy(zone_in, zone, in_sem.at[1]),
@@ -107,6 +91,22 @@
     ]
     for c in loads:
         c.start()
+
+    seam = sizes[1] // 2
+    split = jnp.bool_(sizes[1] >= 4)
+    at_lo, at_hi = (gy == seam - 1) & split, (gy == seam) & split
+    at_seam = at_lo | at_hi
+    barrier = pltpu.get_barrier_semaphore()
+    expected = 0
+    for i, (where, there) in enumerate(spots):
+        far = (at_lo & (DIRS[i][1] > 0)) | (at_hi & (DIRS[i][1] < 0))
+        counts = split & ((where[1] == seam - 1) | (where[1] == seam))
+        beside = there & (far | jnp.logical_not(counts))
+
+        @pl.when(beside)
+        def _():
+            pl.semaphore_signal(barrier, inc=1, device_id=where, device_id_type=MESH)
+        expected = expected + (there & (far | jnp.logical_not(at_seam))).astype(jnp.int32)
 
     for i in range(8):
         @pl.when(jnp.logical_not(spots[i][1]))
@@ -167,11 +167,12 @@
         return tuple(jnp.where(group == z, v, pack) for v, pack in zip(turned, packs)) + tuple(fed_new)
 
     zero, zero8 = jnp.zeros((RX, LY), F32), jnp.zeros((8, LY), F32)
-    packs = lax.fori_loop(0, NZ, own, (zero,) * FIELDS + (zero8,) * 4, unroll=8)
+    packs = lax.fori_loop(0, NZ, own, (zero,) * FIELDS + (zero8,) * 4, unroll=NZ)
     own_fed = packs[FIELDS:]
     packs = packs[:FIELDS]
     k, p, s, q, free = packs
     low8 = low[:8]
+    y_edges = []
     for side_y in range(2):
         if side_y == 0:
             a, b = jnp.where(low, lanes(k, -4), p), jnp.where(low, lanes(s, -4), q)
@@ -182,25 +183,7 @@
         sy[side_y, pl.ds(0, RX)] = a
         sy[side_y, pl.ds(RX, RX)] = b
         sy[side_y, pl.ds(2 * RX, 8)] = m
-        for side_x in range(2):
-            j = 2 * side_y + side_x
-            if side_x == 0:
-                parts_c = (a[:3], b[:2], free[:2])
-            else:
-                parts_c = (a[RX - 3:], b[RX - 2:], free[RX - 2:])
-            sc[j, pl.ds(0, 3)] = parts_c[0]
-            sc[j, pl.ds(3, 2)] = parts_c[1]
-            sc[j, pl.ds(5, 2)] = parts_c[2]
-            sc[j, pl.ds(7, 1)] = parts_c[2][:1]
-
-    def strided(ref, z0, row):
-        return ref.at[pl.ds(z0 * EX + row, NZ, stride=EX)]
-
-    fields = ((perm, 1), (pa, 1), (stor, 0), (rhs, 0), (gain, 0))
-    for n, (f, d) in enumerate(PLANES):
-        ref, z0 = fields[f]
-        sx[0, n] = strided(ref, z0, d)[...]
-        sx[1, n] = strided(ref, z0, RX - 1 - d)[...]
+        y_edges.append((a, b))
 
     def parts(i):
         if i < 2:
@@ -256,10 +239,40 @@
 
     inner = jnp.logical_not(at_seam)
 
+
     @pl.when(at_hi)
     def _():
         pl.semaphore_wait(barrier, expected)
-    send(at_hi, (2, 4, 5), copy)
+    send(at_hi, (2,), copy)
+
+    slot = iota(1, 1) & 7
+    half = slot & 3
+    for side_y, (a, b) in enumerate(y_edges):
+        far_slot = half == (3 if side_y == 0 else 0)
+        back = 3 if side_y == 0 else -3
+        for side_x in range(2):
+            a1, a2, a3 = (v[r:r + 1] for v, r in zip((a,) * 3, (0, 1, 2) if side_x == 0 else (RX - 1, RX - 2, RX - 3)))
+            b1, b2, f1, f2 = (
+                v[r:r + 1] for v, r in zip((b, b, free, free), (0, 1) * 2 if side_x == 0 else (RX - 1, RX - 2) * 2))
+            j = 2 * side_y + side_x
+            sc[j, pl.ds(0, 1)] = jnp.where(far_slot, lanes(a3, back), a1)
+            sc[j, pl.ds(1, 1)] = jnp.where(far_slot, lanes(b2, back), a2)
+            if side_y == 0:
+                masks = jnp.where((slot == 2) | (slot == 3), lanes(f1, -2), jnp.where(slot == 6, lanes(f2, 2), b1))
+            else:
+                masks = jnp.where((slot == 0) | (slot == 1), lanes(f1, -2), jnp.where(slot == 4, lanes(f2, 1), b1))
+            sc[j, pl.ds(2, 1)] = masks
+            sc[j, pl.ds(3, 1)] = a1
+    send(at_hi, (4, 5), copy)
+
+    def strided(ref, z0, row):
+        return ref.at[pl.ds(z0 * EX + row, NZ, stride=EX)]
+
+    fields = ((perm, 1), (pa, 1), (stor, 0), (rhs, 0), (gain, 0))
+    for n, (f, d) in enumerate(PLANES):
+        ref, z0 = fields[f]
+        sx[0, n] = strided(ref, z0, d)[...]
+        sx[1, n] = strided(ref, z0, RX - 1 - d)[...]
 
     loads[6].wait()
     for s in range(NSPEC):
@@ -408,10 +421,18 @@
     strips = []
     for d in range(2):
         minus, plus = rc.at[2 * d], rc.at[2 * d + 1]
-        a = jnp.concatenate([ry[d, pl.ds(0, RX)], plus[pl.ds(0, 3)], pad2, minus[pl.ds(0, 3)]], axis=0)
-        b = jnp.concatenate([ry[d, pl.ds(RX, RX)], plus[pl.ds(3, 2)], pad4, minus[pl.ds(3, 2)]], axis=0)
+        def corner(ref):
+            x, y, z = (ref[pl.ds(n, 1)] for n in range(3))
+            if d == 0:
+                return (x, y, lanes(x, 3)), (z, lanes(y, 3)), (lanes(z, 2), lanes(z, -1))
+            return (x, y, lanes(x, -3)), (z, lanes(y, -3)), (lanes(z, 2), lanes(z, -2))
+
+        (pa1, pa2, pa3), (pb1, pb2), (pm1, pm2) = corner(plus)
+        (ma1, ma2, ma3), (mb1, mb2), (mm1, mm2) = corner(minus)
+        a = jnp.concatenate([ry[d, pl.ds(0, RX)], pa1, pa2, pa3, pad2, ma3, ma2, ma1], axis=0)
+        b = jnp.concatenate([ry[d, pl.ds(RX, RX)], pb1, pb2, pad4, mb2, mb1], axis=0)
         m = ry[d, pl.ds(2 * RX, 8)]
-        m_tail = [plus[pl.ds(5, 2)], pad4, minus[pl.ds(5, 2)]]
+        m_tail = [pm1, pm2, pad4, mm2, mm1]
         if d == 0:
             halos = (a, lanes(a, -4), b, lanes(b, -4), jnp.concatenate([m, lanes(m, -4)] + m_tail, axis=0))
         else:
@@ -527,7 +548,7 @@
     flat, padded, planes = (NZ * EX, LY), ((NZ + 2) * EX, LY), (EX, NZ, LY)
     species, turned = (NSPEC, NZ, RX, LY), (NSPEC, NZ * RX, LY)
     halo = [
-        (2, len(PLANES), NZ, LY), (2, 2 * RX + 8, LY), (4, 8, LY), (2, NSPEC, NZ, LY), (2, NZ, LY),
+        (2, len(PLANES), NZ, LY), (2, 2 * RX + 8, LY), (4, 4, LY), (2, NSPEC, NZ, LY), (2, NZ, LY),
     ]
     vmem = pl.BlockSpec(memory_space=pltpu.VMEM)
     hbm = pl.BlockSpec(memory_space=pltpu.HBM)

time: 22.2 us -> 22 us (level)
  the two profiles are of different devices: /device:TPU:289 before, /device:TPU:30 now
where the time goes in v7:
time: 22 us; the launch traced here: 21.7 us
  Pallas kernels  21.1 us (96%)
  between operations  0.64 us (3%)
    pallas_call x1, Pallas kernels, shards(): pl.pallas_call(lambda *refs: flow_kernel(sizes, *refs), out_shape=[pltpu....  19.6 us
    pallas_call x1, Pallas kernels, shards(): pl.pallas_call(transport_kernel, out_shape=[jax.ShapeDtypeStruct(s, F32)...  1.45 us

profile of v7, /device:TPU:30, one launch (start us, length us, event | category | flops | bytes accessed | tf_op | source)
XLA Modules:
  0.0 21.7 jit_solution(2505956423787015365)
XLA Ops:
  0.6 19.6 %flow.1 = (f32[8,288,128]{2,1,0:T(8,128)S(1)}, f32[8,256,128]{2,1,0:T(8,128)S(1)}, f32[8,256,128]{2,1,0:T(8,128)S(1)}, f32[256,128]{1,0:T(8,128)S(1)}, f32[256,1...) custom-call(f32[8,256,128]{2,1,0:T(8,128)} %bitcast.4, ...), custom_call_target="tpu_custom_call" | custom-call | tf_op jit(solution)/shard_map/flow/pallas_call | solution.py:562
  20.2 1.5 %transport.1 = (f32[8,256,128]{2,1,0:T(8,128)}, f32[256,128]{1,0:T(8,128)}, f32[256,128]{1,0:T(8,128)}) custom-call(f32[8,288,128]{2,1,0:T(8,128)S(1)} %get-tuple-element.14.spx, f32[8,256,128]{2,1,0:T(8,128)S(1)} %get-tuple-element.15.left, f32[8,256,128]{2,1,0:T(8,128)S(1)} %get-tuple-element.16.right, f32[256,128]{1,0:T(8,128)S(1)} %get-tuple-element.17.phi, ...), custom_call_target="tpu_custom_call" | custom-call | tf_op jit(solution)/shard_map/transport/pallas_call | solution.py:580

commit v8 on v7

--- a/solution.py
+++ b/solution.py
@@ -81,13 +81,13 @@
         spots.append(((gx + dx, gy + dy), there))
 
     loads = [
-        pltpu.make_async_copy(sp_in.at[pl.ds(0, 2)], sp.at[pl.ds(0, 2)], in_sem.at[0]),
+        pltpu.make_async_copy(sp_in.at[pl.ds(0, 2)], sp.at[pl.ds(0, 2), pl.ds(0, NZ * RX)], in_sem.at[0]),
         pltpu.make_async_copy(zone_in, zone, in_sem.at[1]),
         pltpu.make_async_copy(por_in, por, in_sem.at[2]),
         pltpu.make_async_copy(old_in, old, in_sem.at[3]),
         pltpu.make_async_copy(src_in, src, in_sem.at[4]),
         pltpu.make_async_copy(fix_in, fix, in_sem.at[5]),
-        pltpu.make_async_copy(sp_in.at[pl.ds(2, NSPEC - 2)], sp.at[pl.ds(2, NSPEC - 2)], in_sem.at[6]),
+        pltpu.make_async_copy(sp_in.at[pl.ds(2, NSPEC - 2)], sp.at[pl.ds(2, NSPEC - 2), pl.ds(0, NZ * RX)], in_sem.at[6]),
     ]
     for c in loads:
         c.start()
@@ -509,7 +509,11 @@
 
 
 def transport_kernel(spx, left, right, phi, rea, final, weight, side, conc_out, p_out, phi_out, conc, sem):
-    outs = [pltpu.make_async_copy(phi, phi_out, sem.at[0]), pltpu.make_async_copy(final, p_out, sem.at[1])]
+    used = pl.ds(0, NZ * RX)
+    outs = [
+        pltpu.make_async_copy(phi.at[used], phi_out, sem.at[0]),
+        pltpu.make_async_copy(final.at[used], p_out, sem.at[1]),
+    ]
     for c in outs:
         c.start()
     lane = iota(RX, 1)
@@ -536,7 +540,7 @@
                     total = total + STOICHIOMETRY[s] * rea[pl.ds(x, NZ, stride=RX)]
                 conc[s, pl.ds(x, NZ, stride=RX)] = total
         some = pl.ds(s0, group)
-        c = pltpu.make_async_copy(conc.at[some], conc_out.at[some], sem.at[2 + s0 // group])
+        c = pltpu.make_async_copy(conc.at[some, used], conc_out.at[some], sem.at[2 + s0 // group])
         c.start()
         outs.append(c)
     for c in outs:
@@ -544,16 +548,16 @@
 
 
 def build(sizes):
-    tile, rows = (NZ, RX, LY), (NZ * RX, LY)
-    flat, padded, planes = (NZ * EX, LY), ((NZ + 2) * EX, LY), (EX, NZ, LY)
-    species, turned = (NSPEC, NZ, RX, LY), (NSPEC, NZ * RX, LY)
+    tile, rows, long_rows = (NZ, RX, LY), (NZ * RX, LY), ((NZ + 1) * RX, LY)
+    flat, padded, planes = ((NZ + 1) * EX, LY), ((NZ + 3) * EX, LY), (EX, NZ, LY)
+    species, turned, long_turned = (NSPEC, NZ, RX, LY), (NSPEC, NZ * RX, LY), (NSPEC, (NZ + 1) * RX, LY)
     halo = [
         (2, len(PLANES), NZ, LY), (2, 2 * RX + 8, LY), (4, 4, LY), (2, NSPEC, NZ, LY), (2, NZ, LY),
     ]
     vmem = pl.BlockSpec(memory_space=pltpu.VMEM)
     hbm = pl.BlockSpec(memory_space=pltpu.HBM)
     middle = [
-        (NSPEC, (RX + 2) * NZ, LY), turned, turned, rows, rows, rows, (7, RX, NZ, LY), (2, NZ, LY),
+        (NSPEC, (RX + 2) * NZ, LY), turned, turned, long_rows, long_rows, long_rows, (7, RX, NZ, LY), (2, NZ, LY),
     ]
     dma = pltpu.SemaphoreType.DMA
 
@@ -566,7 +570,7 @@
             out_specs=[vmem] * len(middle),
             scratch_shapes=[
                 pltpu.VMEM(padded, F32), pltpu.VMEM(planes, F32), pltpu.VMEM((2,) + planes, F32),
-                pltpu.VMEM((2,) + planes, F32), pltpu.VMEM(flat, F32), pltpu.VMEM(turned, F32),
+                pltpu.VMEM((2,) + planes, F32), pltpu.VMEM(flat, F32), pltpu.VMEM(long_turned, F32),
                 pltpu.VMEM(tile, F32), pltpu.VMEM(tile, jnp.int32), pltpu.VMEM(tile, jnp.int32),
                 pltpu.VMEM(tile, F32), pltpu.VMEM(tile, F32),
                 *[pltpu.VMEM(padded, F32)] * 4, *[pltpu.VMEM(flat, F32)] * 3, *[pltpu.VMEM(planes, F32)] * 2,
@@ -582,7 +586,7 @@
             out_shape=[jax.ShapeDtypeStruct(s, F32) for s in (turned, rows, rows)],
             in_specs=[vmem] * len(middle),
             out_specs=[hbm] * 3,
-            scratch_shapes=[pltpu.VMEM(turned, F32), dma((6,))],
+            scratch_shapes=[pltpu.VMEM(long_turned, F32), dma((6,))],
             compiler_params=pltpu.CompilerParams(vmem_limit_bytes=16 * 2**20),
             name="transport",
         )(*shared)

time: 22 us -> 22.1 us (level)
  no operation moved by 1% of the time
where the time goes in v8:
time: 22.1 us; the launch traced here: 21.8 us
  Pallas kernels  21.2 us (96%)
  between operations  0.64 us (3%)
    pallas_call x1, Pallas kernels, shards(): pl.pallas_call(lambda *refs: flow_kernel(sizes, *refs), out_shape=[pltpu....  19.6 us
    pallas_call x1, Pallas kernels, shards(): pl.pallas_call(transport_kernel, out_shape=[jax.ShapeDtypeStruct(s, F32)...  1.6 us

profile of v8, /device:TPU:30, one launch (start us, length us, event | category | flops | bytes accessed | tf_op | source)
XLA Modules:
  0.0 21.8 jit_solution(4645452755242921981)
XLA Ops:
  0.6 19.6 %flow.1 = (f32[8,288,128]{2,1,0:T(8,128)S(1)}, f32[8,256,128]{2,1,0:T(8,128)S(1)}, f32[8,256,128]{2,1,0:T(8,128)S(1)}, f32[272,128]{1,0:T(8,128)S(1)}, f32[272,1...) custom-call(f32[8,256,128]{2,1,0:T(8,128)} %bitcast.4, ...), custom_call_target="tpu_custom_call" | custom-call | tf_op jit(solution)/shard_map/flow/pallas_call | solution.py:566
  20.2 1.6 %transport.1 = (f32[8,256,128]{2,1,0:T(8,128)}, f32[256,128]{1,0:T(8,128)}, f32[256,128]{1,0:T(8,128)}) custom-call(f32[8,288,128]{2,1,0:T(8,128)S(1)} %get-tuple-element.14.spx, f32[8,256,128]{2,1,0:T(8,128)S(1)} %get-tuple-element.15.left, f32[8,256,128]{2,1,0:T(8,128)S(1)} %get-tuple-element.16.right, f32[272,128]{1,0:T(8,128)S(1)} %get-tuple-element.17.phi, ...), custom_call_target="tpu_custom_call" | custom-call | tf_op jit(solution)/shard_map/transport/pallas_call | solution.py:584
